TPU v7x, 128 devices: a whole 4x4x4 slice. The times are simulated.
128 devices in a mesh: pool: 4 (over z), group: 4 (over x), tensor: 8 (over y, core).
Axes of the slice: x: 4, y: 4, z: 4, core: 2. Of those that a mesh axis runs over, the one named last changes fastest.
Arguments:
- tokens: bfloat16 [4, 2048, 8192], P('group', 'pool'), may hold values from -6 to 6
- input_norm_gain: bfloat16 [8192], replicated, may hold values from 0.5 to 1.5
- query_projection: bfloat16 [8192, 8192], P(None, 'tensor'), may hold values from -0.0625 to 0.0625
- key_projection: bfloat16 [8192, 1024], P(None, 'tensor'), may hold values from -0.0625 to 0.0625
- value_projection: bfloat16 [8192, 1024], P(None, 'tensor'), may hold values from -0.0625 to 0.0625
- query_bias_vector: bfloat16 [8192], P('tensor'), may hold values from -8 to 8
- key_bias_vector: bfloat16 [1024], P('tensor'), may hold values from -8 to 8
- value_bias_vector: bfloat16 [1024], P('tensor'), may hold values from -3 to 3
- adapter_down_factors: bfloat16 [32, 3, 64, 8192], P(('pool', 'group'), None, None, 'tensor'), may hold values from -0.0625 to 0.0625
- adapter_up_query: bfloat16 [32, 64, 8192], P(('pool', 'group'), None, 'tensor'), may hold values from -0.19921875 to 0.19921875
- adapter_up_key: bfloat16 [32, 64, 1024], P(('pool', 'group'), None, 'tensor'), may hold values from -0.19921875 to 0.19921875
- adapter_up_value: bfloat16 [32, 64, 1024], P(('pool', 'group'), None, 'tensor'), may hold values from -0.19921875 to 0.19921875
- group_adapter_ids: int32 [4], replicated, may hold values from 0 to 31
- lengths: int32 [4, 3], P('group'), may hold values from 1 to 1024, 2048 in all within a row
- page_slot_table: int32 [512], replicated, may hold values from 0 to 511, as said below
Outputs:
- attn_out: bfloat16 [4, 2048, 8192], P('group', 'pool', 'tensor')
- kv_store: bfloat16 [512, 8, 2, 16, 128], P(('pool', 'group'), 'tensor')
Inputs may be any that keep to these rules, and one draw needn't show every extreme that they name: `page_slot_table`: A permutation of the 512 storage slots; slot s lies on owner s // 32, where the device at pool index a and group index b is owner a * 4 + b. The 32 pages whose tokens one index of pool holds within one group map exactly 2 to each owner.
All inputs are finite; a program needn't handle non-finite values.
Results may differ from a plain program's by a relative error of at most 0.012.
Values may be sent and summed in bfloat16 or wider, within the bound.
A program may use at most 192 MiB of HBM per device.

v0:
```python
import jax
import jax.numpy as jnp
from jax import lax
from jax.sharding import PartitionSpec as P

HEAD_SIZE = 128
PAGE_TOKENS = 16


adapter_scale = 2.0
rope_theta = 1000000.0
norm_eps = 1e-06


def request_positions(lengths_row, token_count):
    request_end = jnp.cumsum(lengths_row)
    starts = request_end - lengths_row
    token_index = jnp.arange(token_count, dtype=jnp.int32)
    group_member = (token_index[:, None] >= starts[None, :]) & (
        token_index[:, None] < request_end[None, :]
    )
    numbers = jnp.arange(lengths_row.shape[0], dtype=jnp.int32)
    segment = jnp.sum(jnp.where(group_member, numbers[None, :], 0), axis=1)
    page_offset = token_index - jnp.sum(jnp.where(group_member, starts[None, :], 0), axis=1)
    return (segment, page_offset)


def apply_rotation(vectors, page_offset):
    half_dim = vectors.shape[-1] // 2
    frequency = rope_theta ** (-(jnp.arange(half_dim, dtype=jnp.float32) * 2.0 / vectors.shape[-1]))
    angle = page_offset.astype(jnp.float32)[:, None] * frequency[None, :]
    cosine = jnp.cos(angle)[:, None, :]
    sine_part = jnp.sin(angle)[:, None, :]
    first_half = vectors[..., :half_dim]
    second = vectors[..., half_dim:]
    return jnp.concatenate(
        [first_half * cosine - second * sine_part, second * cosine + first_half * sine_part],
        axis=-1,
    )


def rms_normalize(rows, input_norm_gain):
    widened = rows.astype(jnp.float32)
    row_scale = lax.rsqrt(jnp.mean(widened * widened, axis=-1, keepdims=True) + norm_eps)
    return (widened * row_scale * input_norm_gain.astype(jnp.float32)).astype(jnp.bfloat16)


def per_device(
    tokens,
    input_norm_gain,
    query_projection,
    key_projection,
    value_projection,
    query_bias_vector,
    key_bias_vector,
    value_bias_vector,
    adapter_down_factors,
    adapter_up_query,
    adapter_up_key,
    adapter_up_value,
    group_adapter_ids,
    lengths,
    page_slot_table,
):
    pool_count = lax.axis_size("pool")
    group_count = lax.axis_size("group")
    owners = pool_count * group_count
    my_owner = lax.axis_index("pool") * group_count + lax.axis_index("group")
    slot_on_shard = adapter_down_factors.shape[0]
    chooser = (
        (group_adapter_ids - my_owner * slot_on_shard)[:, None]
        == jnp.arange(slot_on_shard, dtype=jnp.int32)[None, :]
    ).astype(jnp.bfloat16)

    def select_adapter_slot(bank):
        bank_rows = bank.reshape(slot_on_shard, -1)
        picked = jnp.dot(chooser, bank_rows, preferred_element_type=jnp.float32).astype(
            jnp.bfloat16
        )
        return picked.reshape((chooser.shape[0],) + bank.shape[1:])

    contributions = (
        select_adapter_slot(adapter_down_factors),
        select_adapter_slot(adapter_up_query),
        select_adapter_slot(adapter_up_key),
        select_adapter_slot(adapter_up_value),
    )
    fetched = (
        lax.psum(contributions[0], ("pool", "group")).astype(jnp.float32),
        lax.psum(contributions[1], ("pool", "group")).astype(jnp.float32),
        lax.psum(contributions[2], ("pool", "group")).astype(jnp.float32),
        lax.psum(contributions[3], ("pool", "group")).astype(jnp.float32),
    )
    own_parts = [
        lax.dynamic_index_in_dim(group_member, lax.axis_index("group"), 0, keepdims=False)
        for group_member in fetched
    ]
    down_own, up_query, up_key, up_value = [
        group_member.astype(jnp.bfloat16) for group_member in own_parts
    ]
    shard_part = lax.all_gather(down_own, "tensor", axis=2, tiled=True)
    pieces_out = []
    for group_member, (frozen_weight, up_factor) in enumerate(
        ((query_projection, up_query), (key_projection, up_key), (value_projection, up_value))
    ):
        weight_update = jnp.dot(
            shard_part[group_member].T, up_factor, preferred_element_type=jnp.float32
        )
        pieces_out.append(
            (frozen_weight.astype(jnp.float32) + adapter_scale * weight_update).astype(jnp.bfloat16)
        )
    merged_weight = jnp.concatenate(pieces_out, axis=1)
    normed = rms_normalize(tokens[0], input_norm_gain)
    projected = jnp.dot(normed, merged_weight, preferred_element_type=jnp.float32)
    query_cols = query_projection.shape[1]
    key_cols = key_projection.shape[1]
    tok_dev = tokens.shape[1]
    heads_kv = key_cols // HEAD_SIZE
    query_per_key_ratio = query_cols // key_cols
    segment, page_offset = request_positions(lengths[0], tok_dev * pool_count)
    first_token = lax.axis_index("pool") * tok_dev
    my_index = first_token + jnp.arange(tok_dev, dtype=jnp.int32)
    my_segment = lax.dynamic_slice_in_dim(segment, first_token, tok_dev)
    my_offset = lax.dynamic_slice_in_dim(page_offset, first_token, tok_dev)
    query_raw = (projected[:, :query_cols] + query_bias_vector.astype(jnp.float32)).reshape(
        tok_dev, query_cols // HEAD_SIZE, HEAD_SIZE
    )
    query_rows = (
        (apply_rotation(query_raw, my_offset) * HEAD_SIZE ** (-0.5))
        .astype(jnp.bfloat16)
        .reshape(tok_dev, heads_kv, query_per_key_ratio, HEAD_SIZE)
    )
    key_unrotated = (
        projected[:, query_cols : query_cols + key_cols] + key_bias_vector.astype(jnp.float32)
    ).reshape(tok_dev, heads_kv, HEAD_SIZE)
    key_rotated = apply_rotation(key_unrotated, my_offset).astype(jnp.bfloat16)
    value_row_block = (
        (projected[:, query_cols + key_cols :] + value_bias_vector.astype(jnp.float32))
        .reshape(tok_dev, heads_kv, HEAD_SIZE)
        .astype(jnp.bfloat16)
    )
    running = jnp.full((heads_kv, query_per_key_ratio, tok_dev), -1e30, jnp.float32)
    key_piece = lax.all_gather(key_rotated, "pool", axis=0, tiled=True)
    value_piece = lax.all_gather(value_row_block, "pool", axis=0, tiled=True)
    block_rows = key_piece.shape[0]
    key_index = jnp.arange(block_rows, dtype=jnp.int32)
    allowed = (my_segment[:, None] == segment[None, :]) & (key_index[None, :] <= my_index[:, None])
    scores = jnp.einsum("tkgd,skd->kgts", query_rows, key_piece, preferred_element_type=jnp.float32)
    scores = jnp.where(allowed, scores, -1e30)
    new_top = jnp.maximum(running, jnp.max(scores, axis=-1))
    weights = jnp.where(allowed, jnp.exp(scores - new_top[..., None]), 0.0).astype(jnp.bfloat16)
    row_total = jnp.sum(weights.astype(jnp.float32), axis=-1)
    weighted = jnp.einsum(
        "kgts,skd->kgtd", weights, value_piece, preferred_element_type=jnp.float32
    )
    running, row_total, weighted = (new_top, row_total, weighted)
    mixed = (
        (weighted / row_total[..., None])
        .transpose(2, 0, 1, 3)
        .reshape(1, tok_dev, query_cols)
        .astype(jnp.bfloat16)
    )
    pages_dev = tok_dev // PAGE_TOKENS
    page_cap = pages_dev // owners
    stacked_factors = jnp.stack([key_rotated, value_row_block], axis=1).reshape(
        pages_dev, PAGE_TOKENS, 2, heads_kv, HEAD_SIZE
    )
    page_rows = stacked_factors.transpose(0, 3, 2, 1, 4).reshape(pages_dev, -1)
    slot_table = (
        page_slot_table.reshape(group_count, pool_count, pages_dev)
        .transpose(1, 0, 2)
        .reshape(owners, pages_dev)
    )
    target_owner = slot_table // pages_dev
    page_number = jnp.arange(pages_dev, dtype=jnp.int32)
    own_targets = lax.dynamic_index_in_dim(target_owner, my_owner, 0, keepdims=False)
    earlier = (own_targets[:, None] == own_targets[None, :]) & (
        page_number[None, :] < page_number[:, None]
    )
    arrival = jnp.sum(earlier.astype(jnp.int32), axis=1)
    position = own_targets * page_cap + arrival
    sender = (page_number[:, None] == position[None, :]).astype(jnp.bfloat16)
    outgoing = (
        jnp.dot(sender, page_rows, preferred_element_type=jnp.float32)
        .astype(jnp.bfloat16)
        .reshape(owners, page_cap, -1)
    )
    received = lax.all_to_all(outgoing, ("pool", "group"), split_axis=0, concat_axis=0, tiled=True)
    received = received.reshape(owners * page_cap, -1)
    mine_all = target_owner == my_owner
    before_all = (target_owner[:, :, None] == target_owner[:, None, :]) & (
        page_number[None, None, :] < page_number[None, :, None]
    )
    arrival_all = jnp.sum(before_all.astype(jnp.int32), axis=2)
    item_number = jnp.arange(owners, dtype=jnp.int32)[:, None] * page_cap + arrival_all
    local_slot = slot_table - my_owner * pages_dev
    placer = (
        (local_slot.reshape(-1)[None, :] == page_number[:, None]) & mine_all.reshape(-1)[None, :]
    ).astype(jnp.float32)
    arrivals = (
        item_number.reshape(-1)[:, None] == jnp.arange(owners * page_cap, dtype=jnp.int32)[None, :]
    ).astype(jnp.float32)
    placement = jnp.dot(placer, arrivals, preferred_element_type=jnp.float32).astype(jnp.bfloat16)
    stored = jnp.dot(placement, received, preferred_element_type=jnp.float32).astype(jnp.bfloat16)
    stored = stored.reshape(pages_dev, heads_kv, 2, PAGE_TOKENS, HEAD_SIZE)
    return (mixed, stored)


def solution(mesh):
    placed = (
        P("group", "pool", None),
        P(),
        P(None, "tensor"),
        P(None, "tensor"),
        P(None, "tensor"),
        P("tensor"),
        P("tensor"),
        P("tensor"),
        P(("pool", "group"), None, None, "tensor"),
        P(("pool", "group"), None, "tensor"),
        P(("pool", "group"), None, "tensor"),
        P(("pool", "group"), None, "tensor"),
        P(),
        P("group", None),
        P(),
    )
    return jax.shard_map(
        per_device,
        mesh=mesh,
        in_specs=placed,
        out_specs=(P("group", "pool", "tensor"), P(("pool", "group"), "tensor", None, None, None)),
        check_vma=False,
    )
```

profile of v0, /device:TPU:64, one launch (start us, length us, event | category | flops | bytes accessed | tf_op | source)
XLA Modules:
  0.0 272.2 jit_solution(11107271735047385690)
XLA Ops:
  7.2 0.7 broadcast_subtract_fusion.1
  7.9 1.0 fusion.24
  8.9 1.0 fusion.25
  9.9 1.9 copy.65
  11.8 1.0 convolution_convert_fusion
  12.9 1.6 copy.66
  14.5 0.3 copy.67
  14.7 0.5 convolution_convert_fusion.1
  15.2 1.0 copy.90
  16.2 0.7 copy_bitcast_fusion.1
  16.9 0.2 all-gather.4.cloned.1.call-start
  17.1 91.3 %all-reduce.3.cloned.1.call-done = (bf16[4,3,64,1024]{3,2,1,0:T(8,128)(2,1)}, bf16[4,64,128]{2,1,0:T(8,128)(2,1)}, bf16[4,64,128]{2,1,0:T(8,128)(2,1)}, bf16[4,64,1024]{2,1,0:T(8,128)(2,1)}) async-done(((bf16[4,3,64,1024]{3,2,1,0:T(8,128)(2,1)}, bf16[4,64,128]{2,1,0:T(8,128)(2,1)}, bf16[4,64,128]{2,1,0:T(8,128)(2,1)}, bf16[4,64,1024]{2,1,0:T(8,128)(2,1)}), (bf16[4,3,64,1024]{3,2,1,0:T(8,128)(2,1)}, ...) | async-done | bytes 2228240 | tf_op jit(solution)/shard_map/psum | solution.py:89
  108.4 1.8 convert_convert_fusion
  110.2 21.3 %copy.46 = bf16[8192,1024]{0,1:T(8,128)(2,1)} copy(bf16[8192,1024]{1,0:T(8,128)(2,1)} %param.17) | data formatting | bytes 33554432 | tf_op args[2]
  131.6 3.0 %copy.47 = bf16[8192,128]{0,1:T(8,128)(2,1)} copy(bf16[8192,128]{1,0:T(8,128)(2,1)S(1)} %copy-done.1) | data formatting | bytes 4194304 | tf_op args[3]
  134.5 2.9 %copy.48 = bf16[8192,128]{0,1:T(8,128)(2,1)S(1)} copy(bf16[8192,128]{1,0:T(8,128)(2,1)} %param.19) | data formatting | bytes 4194304 | tf_op args[4]
  137.5 0.2 reduce-window.4
  137.9 0.5 convert_reduce_fusion.1
  138.5 0.1 select_reduce_fusion.1
  138.9 0.2 convert_reduce_fusion.2
  139.1 5.1 %fusion.7 = f32[512]{0:T(512)S(1)} fusion(bf16[1,512,8192]{2,1,0:T(8,128)(2,1)} %param.15), kind=kLoop, calls=%fused_computation.15 | loop fusion | flops 12582400 | bytes 8390656 | tf_op jit(solution)/shard_map/reduce_sum | solution.py:44
  144.2 1.8 multiply_cosine_fusion
  146.0 0.9 fusion.20
  146.9 11.8 %add_convert_fusion = bf16[8192,1024]{0,1:T(8,128)(2,1)} fusion(bf16[8192,1024]{0,1:T(8,128)(2,1)} %copy.46, bf16[1,3,64,8192]{3,2,1,0:T(8,128)(2,1)} %all-gather.4.cloned.1.call-done, bf16[4,64,1024]{2,1,0:T(8,128)(2,1)} %get-tuple-element.15, s32[]{:T(128)S(6)} %select_n.52), kind=kOutput, calls=%fused_computation.5 | convolution fusion | flops 1107427328 | bytes 34734084 | tf_op jit(solution)/shard_map/dot_general | solution.py:106
  158.7 2.7 fusion.14
  161.4 3.3 %fusion.15 = bf16[8192,128]{0,1:T(8,128)(2,1)} fusion(bf16[8192,128]{0,1:T(8,128)(2,1)S(1)} %copy.48, bf16[1,3,64,8192]{3,2,1,0:T(8,128)(2,1)} %all-gather.4.cloned.1.call-done, bf16[4,64,128]{2,1,0:T(8,128)(2,1)} %get-tuple-element.13, s32[]{:T(128)S(6)} %select_n.52), kind=kOutput, calls=%fused_computation.25 | convolution fusion | flops 138428416 | bytes 5259268 | tf_op jit(solution)/shard_map/dot_general | solution.py:106
  164.8 14.8 %fusion.1 = f32[512,1280]{1,0:T(8,128)S(1)} fusion(bf16[8192,128]{0,1:T(8,128)(2,1)} %fusion.15, bf16[8192,128]{0,1:T(8,128)(2,1)S(1)} %fusion.14, bf16[8192,1024]{0,1:T(8,128)(2,1)} %add_convert_fusion, bf16[1,512,8192]{2,1,0:T(8,128)(2,1)} %param.15, f32[8192]{0:T(1024)S(1)} %convert_element_type.166, f32[512]{0:T(512)S(1)} %add_rsqrt_fusion), kind=kOutput, calls=%fused_computation.9 | convolution fusion | flops 10817110016 | bytes 32016384 | tf_op jit(solution)/shard_map/dot_general | solution.py:114
  179.6 1.5 copy-done
  181.1 1.2 fusion.38
  182.4 13.4 %all-gather.1 = bf16[2048,128]{1,0:T(8,128)(2,1)S(1)} all-gather(bf16[512,128]{1,0:T(8,128)(2,1)S(1)} %get-tuple-element.18), channel_id=3, replica_groups=mesh['pool'=4,'group'=4,'tensor'=8] {'pool'}, dimensions={0}, use_global_device_ids=true | all-gather | bytes 655360 | tf_op jit(solution)/shard_map/all_gather | solution.py:144
  195.8 0.1 pad_maximum_fusion
  195.9 0.1 maximum_bitcast_fusion
  196.0 0.1 reshape.448
  196.2 0.2 convolution_convert_fusion.5
  196.4 0.9 reshape.449
  197.3 6.6 %all-to-all-start = ((bf16[16,2,4096]{2,1,0:T(2,128)(2,1)}), bf16[16,2,4096]{2,1,0:T(2,128)(2,1)S(1)}, u32[]{:S(2)}, u32[]{:S(2)}) async-start(bf16[16,2,4096]{2,1,0:T(2,128)(2,1)} %reshape.449), calls=%async_computation | async-start | bytes 524288 | tf_op jit(solution)/shard_map/all_to_all | solution.py:188
  203.9 13.0 %all_gather.10 = bf16[2048,1,128]{2,0,1:T(8,128)(2,1)S(1)} all-gather(bf16[512,1,128]{2,0,1:T(8,128)(2,1)S(1)} %pad_maximum_fusion), channel_id=1, replica_groups=mesh['pool'=4,'group'=4,'tensor'=8] {'pool'}, dimensions={0}, use_global_device_ids=true | all-gather | bytes 655360 | tf_op jit(solution)/shard_map/all_gather | solution.py:143
  217.0 1.8 fusion.21
  218.8 0.5 copy.73
  219.3 0.7 fusion.86
  219.9 0.3 copy-done.2
  220.2 0.7 multiply_subtract_fusion
  221.0 13.4 %fusion = (f32[8,512]{1,0:T(8,128)S(1)}, f32[2048,512,8]{1,0,2:T(8,128)}) fusion(pred[512,2048]{0,1:T(8,128)(4,1)S(1)} %fusion.20, f32[512,8,64]{2,0,1:T(8,128)S(1)} %get-tuple-element.17, f32[512,8,64]{2,0,1:T(8,128)S(1)} %get-tuple-element.16, bf16[2048,1,128]{2,0,1:T(8,128)(2,1)S(1)} %all_gather.10), kind=kOutput, calls=%fused_computation.6 | convolution fusion | flops 2165829632 | bytes 37240832 | tf_op jit(solution)/shard_map/tkgd,skd->kgts/dot_general | solution.py:148
  234.4 14.4 %convert_reduce_fusion = f32[8,512]{1,0:T(8,128)S(1)} fusion(f32[8,512]{1,0:T(8,128)S(1)} %broadcast_maximum_fusion, f32[2048,512,8]{1,0,2:T(8,128)} %get-tuple-element.27, pred[512,2048]{0,1:T(8,128)(4,1)S(1)} %fusion.20), kind=kLoop, calls=%fused_computation.3 | loop fusion | flops 50327552 | bytes 34635776 | tf_op jit(solution)/shard_map/reduce_sum | solution.py:152
  248.8 13.9 %divide_convert_fusion = bf16[8,512,128]{1,2,0:T(8,128)(2,1)S(1)} fusion(f32[8,512]{1,0:T(8,128)S(1)} %convert_reduce_fusion, bf16[2048,128]{1,0:T(8,128)(2,1)S(1)} %all-gather.1, f32[2048,512,8]{1,0,2:T(8,128)} %get-tuple-element.27, f32[8,512]{1,0:T(8,128)S(1)} %broadcast_maximum_fusion, pred[512,2048]{0,1:T(8,128)(4,1)S(1)} %fusion.20), kind=kOutput, calls=%fused_computation.39 | convolution fusion | flops 2182086656 | bytes 36208640 | tf_op jit(solution)/shard_map/kgts,skd->kgtd/dot_general | solution.py:153
  262.7 1.3 copy.58
  264.1 0.4 fusion.23
  264.6 0.7 copy.74
  (48 shorter events, 0.9 us)
Async XLA Ops:
  7.2 101.3 %all-reduce.3.cloned.1.call-start = ((), (), s32[]{:S(2)}) async-start(), calls=%async_computation.2 | async-start | bytes 4456448 | tf_op jit(solution)/shard_map/psum | solution.py:89
  11.8 2.7 copy-start.3
  16.9 130.1 %all-gather.4.cloned.1.call-start = ((), (), s32[]{:S(2)}) async-start(), calls=%async_computation.1 | async-start | bytes 3538944 | tf_op jit(solution)/shard_map/all_gather | solution.py:101
  110.2 21.3 %copy-start.1 = (bf16[8192,128]{1,0:T(8,128)(2,1)S(1)}, bf16[8192,128]{1,0:T(8,128)(2,1)}, u32[]{:S(2)}) copy-start(bf16[8192,128]{1,0:T(8,128)(2,1)} %param.18) | copy-start | bytes 6291460
  131.5 5.9 %copy-start.4 = (bf16[8192]{0:T(1024)(128)(2,1)S(1)}, bf16[8192]{0:T(1024)(128)(2,1)}, u32[]{:S(2)}) copy-start(bf16[8192]{0:T(1024)(128)(2,1)} %param.16) | copy-start | bytes 49156
  131.5 6.0 %copy-start.7 = (bf16[128]{0:T(256)(128)(2,1)S(1)}, bf16[128]{0:T(256)(128)(2,1)}, u32[]{:S(2)}) copy-start(bf16[128]{0:T(256)(128)(2,1)} %param.21) | copy-start | bytes 772
  131.5 6.0 %copy-start.8 = (bf16[128]{0:T(256)(128)(2,1)S(1)}, bf16[128]{0:T(256)(128)(2,1)}, u32[]{:S(2)}) copy-start(bf16[128]{0:T(256)(128)(2,1)} %param.22) | copy-start | bytes 772
  131.5 6.0 %copy-start.9 = (s32[1,3]{1,0:T(1,128)S(1)}, s32[1,3]{1,0:T(1,128)}, u32[]{:S(2)}) copy-start(s32[1,3]{1,0:T(1,128)} %param.28) | copy-start | bytes 40
  131.5 6.2 %copy-start.5 = (s32[512]{0:T(512)S(1)}, s32[512]{0:T(512)}, u32[]{:S(2)}) copy-start(s32[512]{0:T(512)} %param.29) | copy-start | bytes 6148
  131.6 7.0 %copy-start.6 = (bf16[1024]{0:T(1024)(128)(2,1)S(1)}, bf16[1024]{0:T(1024)(128)(2,1)}, u32[]{:S(2)}) copy-start(bf16[1024]{0:T(1024)(128)(2,1)} %param.20) | copy-start | bytes 6148
  179.6 1.5 copy-start
  197.3 66.7 %all-to-all-start = ((bf16[16,2,4096]{2,1,0:T(2,128)(2,1)}), bf16[16,2,4096]{2,1,0:T(2,128)(2,1)S(1)}, u32[]{:S(2)}, u32[]{:S(2)}) async-start(bf16[16,2,4096]{2,1,0:T(2,128)(2,1)} %reshape.449), calls=%async_computation | async-start | bytes 524288 | tf_op jit(solution)/shard_map/all_to_all | solution.py:188
  219.3 1.0 copy-start.2
Sparse Core Ops, SparseCore 0:
  17.0 91.3 all-reduce.2
  110.7 28.7 all-gather.3
where the time goes:
time: 276 us; the launch traced here: 272 us
  waiting for transfers between devices  91.4 us (33%)
  matrix products  64.1 us (23%)
  local copies, waits for them, and re-layouts  39.1 us (14%)
  other arithmetic  29.8 us (11%)
  blocking collectives  26.5 us (10%)
  between operations  14.4 us (5%)
  starting transfers between devices  6.9 us (2%)
    psum x1, waiting for transfers between devices, per_device(): lax.psum(contributions[0], ('pool', 'group')).astype(jnp.float32)  91.3 us
    unnamed x30, local copies, waits for them, and re-layouts  36.3 us
    dot_general x3, matrix products, per_device(): jnp.dot(shard_part[group_member].T, up_factor, preferred_element_type=jnp...  17.8 us
    dot_general x1, matrix products, per_device(): jnp.dot(normed, merged_weight, preferred_element_type=jnp.float32)  14.8 us
    reduce_sum x1, other arithmetic, per_device(): row_total = jnp.sum(weights.astype(jnp.float32), axis=-1)  14.4 us
    dot_general x1, matrix products, per_device(): jnp.einsum('kgts,skd->kgtd', weights, value_piece, preferred_element_type...  13.9 us
    all_gather x1, blocking collectives, per_device(): value_piece = lax.all_gather(value_row_block, 'pool', axis=0, tiled=True)  13.4 us
    dot_general x1, matrix products, per_device(): jnp.einsum('tkgd,skd->kgts', query_rows, key_piece, preferred_element_typ...  13.4 us
  transfers between devices with their start and end apart: 3, of which 1 were waited for; matrix products, arithmetic and copies ran while one was open for 31% of the time, Pallas kernels for 0%

commit v1 on v0

v1 whole, which is shorter than its diff:
```python
import functools
import math

import jax
import jax.numpy as jnp
import numpy as np
from jax import lax
from jax.experimental import pallas as pl
from jax.experimental.pallas import tpu as pltpu
from jax.sharding import PartitionSpec as P

HEAD = 128
PAGE = 16
RANK = 64
ADAPTER_SCALE = 2.0
ROPE_THETA = 1000000.0
EPS = 1e-06
MASKED = -1e30
BF = jnp.bfloat16
F32 = jnp.float32
MESH = pl.DeviceIdType.MESH
POOL = 4
GROUP = 4
OWNERS = 16
TENSOR = 8
TOK = 512
WIDTH = 8192
CHUNK = 1024
QCOLS = 1024
HEADS = 8
QB = 256
KWIN = 1280

IDS, LEN, SEND, RECV = 0, 4, 8, 40


def dot(a, b):
    return jnp.dot(a, b, preferred_element_type=F32)


def dot_t(a, b):
    return lax.dot_general(a, b, (((1,), (1,)), ((), ())), preferred_element_type=F32)


def kernel(
    tab, tokens, gain, wq, wk, wv, bias, down, upq, upk, upv, rope,
    out, store,
    x, wkv_b, wq_b, acc_kv, acc_q, sq, rsb, rope_b, cosb, sinb,
    r1kv, r1u, r1q, st_kv, st_u, st_q, dkv, upkv, dq, zst, zr, zs, zf,
    kvo, kvp, pst, prv, qbuf, qext, kext, kt,
    tok_sem, wkv_sem, wq_sem, rope_sem, loc_sem,
    s1kv, s1u, s1q, s2kv, s2u, s2q, srs, sag, skv, spg,
    r1kv_s, r1u_s, r1q_s, r2kv_s, r2u_s, r2q_s, rrs, rag, rkv, rpg,
):
    me_p = lax.axis_index("pool")
    me_g = lax.axis_index("group")
    me_t = lax.axis_index("tensor")
    owner = me_p * GROUP + me_g

    def tok_copy(c):
        return pltpu.make_async_copy(
            tokens.at[0, :, pl.ds(pl.multiple_of(c * CHUNK, CHUNK), CHUNK)], x.at[c], tok_sem.at[c]
        )

    def wkv_copy(c, which):
        src = (wk, wv)[which]
        return pltpu.make_async_copy(
            src.at[pl.ds(pl.multiple_of(c * CHUNK, CHUNK), CHUNK), :],
            wkv_b.at[c, :, pl.ds(which * HEAD, HEAD)],
            wkv_sem.at[c, which],
        )

    def wq_copy(j):
        return pltpu.make_async_copy(
            wq.at[:, pl.ds(j * 256, 256)], wq_b.at[j], wq_sem.at[j]
        )

    rope_copy = pltpu.make_async_copy(rope, rope_b, rope_sem)

    upkv[...] = jnp.zeros_like(upkv)
    dq[...] = jnp.zeros_like(dq)

    barrier = pltpu.get_barrier_semaphore()

    def plane(i):
        dest = lax.rem(owner + i, OWNERS)
        return dest // GROUP, lax.rem(dest, GROUP)

    @pl.loop(1, OWNERS)
    def _(i):
        dp, dg = plane(i)
        pl.semaphore_signal(barrier, inc=1, device_id=(dp, dg, me_t), device_id_type=MESH)

    @pl.loop(1, TENSOR)
    def _(i):
        dt = lax.rem(me_t + i, TENSOR)
        pl.semaphore_signal(barrier, inc=1, device_id=(me_p, me_g, dt), device_id_type=MESH)

    for c in range(2):
        tok_copy(c).start()
        wkv_copy(c, 0).start()
        wkv_copy(c, 1).start()

    pl.semaphore_wait(barrier, OWNERS - 1 + TENSOR - 1)

    def piece(i):
        dp, dg = plane(i)
        return dp, dg, pl.ds(pl.multiple_of(dp * 16, 16), 16), pl.ds(pl.multiple_of(dg * 256, 256), 256)

    mine2 = pl.ds(owner * 2, 2)
    my_rows = pl.ds(pl.multiple_of(me_p * 16, 16), 16)
    my_cols = pl.ds(pl.multiple_of(me_g * 256, 256), 256)

    def remote(src, dst, send, recv, dp, dg, dt):
        return pltpu.make_async_remote_copy(
            src_ref=src, dst_ref=dst, send_sem=send, recv_sem=recv,
            device_id=(dp, dg, dt), device_id_type=MESH,
        )

    def p1kv(i):
        dp, dg, rows, cols = piece(i)
        return remote(down.at[:, pl.ds(1, 2), rows, cols], r1kv.at[mine2], s1kv.at[i], r1kv_s.at[i], dp, dg, me_t)

    def p1q(i):
        dp, dg, rows, cols = piece(i)
        return (
            remote(down.at[:, 0, rows, cols], r1q.at[mine2, 0], s1q.at[0, i], r1q_s.at[0, i], dp, dg, me_t),
            remote(upq.at[:, rows, cols], r1q.at[mine2, 1], s1q.at[1, i], r1q_s.at[1, i], dp, dg, me_t),
        )

    def p1u(i):
        dp, dg, rows, _ = piece(i)
        return (
            remote(upk.at[:, rows, :], r1u.at[mine2, 0], s1u.at[0, i], r1u_s.at[0, i], dp, dg, me_t),
            remote(upv.at[:, rows, :], r1u.at[mine2, 1], s1u.at[1, i], r1u_s.at[1, i], dp, dg, me_t),
        )

    own1 = (
        pltpu.make_async_copy(down.at[:, pl.ds(1, 2), my_rows, my_cols], r1kv.at[mine2], loc_sem.at[0]),
        pltpu.make_async_copy(upk.at[:, my_rows, :], r1u.at[mine2, 0], loc_sem.at[1]),
        pltpu.make_async_copy(upv.at[:, my_rows, :], r1u.at[mine2, 1], loc_sem.at[2]),
        pltpu.make_async_copy(down.at[:, 0, my_rows, my_cols], r1q.at[mine2, 0], loc_sem.at[3]),
        pltpu.make_async_copy(upq.at[:, my_rows, my_cols], r1q.at[mine2, 1], loc_sem.at[4]),
    )

    @pl.loop(1, OWNERS)
    def _(i):
        p1kv(i).start()

    def to_column_zero(act):
        @pl.loop(0, POOL)
        def _(dp):
            i = lax.rem(dp * GROUP - owner + OWNERS, OWNERS)

            @pl.when(i != 0)
            def _():
                act(i)

    def from_column_zero(act):
        @pl.loop(0, POOL)
        def _(sp):
            i = lax.rem(owner - sp * GROUP + OWNERS, OWNERS)

            @pl.when(i != 0)
            def _():
                act(i)

    def start_both(pair):
        pair[0].start()
        pair[1].start()

    to_column_zero(lambda i: start_both(p1u(i)))
    for cp in own1:
        cp.start()

    @pl.loop(1, OWNERS)
    def _(i):
        start_both(p1q(i))

    for c in range(2, 8):
        tok_copy(c).start()
        wkv_copy(c, 0).start()
        wkv_copy(c, 1).start()
    rope_copy.start()
    for j in range(4):
        wq_copy(j).start()

    sq[...] = jnp.zeros_like(sq)
    acc_kv[...] = jnp.zeros_like(acc_kv)

    @pl.when(me_p < 1)
    def _():
        kvp[1] = jnp.zeros(kvp.shape[1:], BF)

    @pl.when(me_p < 2)
    def _():
        kvp[0] = jnp.zeros(kvp.shape[1:], BF)

    @pl.loop(0, 8)
    def _(c):
        tok_copy(c).wait()
        wkv_copy(c, 0).wait()
        wkv_copy(c, 1).wait()

        @pl.loop(0, TOK // 64)
        def _(r):
            rows = pl.ds(pl.multiple_of(r * 64, 64), 64)
            raw = x[c, rows, :].astype(F32)
            s = sq[rows, :]
            for k in range(CHUNK // 128):
                part = raw[:, k * 128 : (k + 1) * 128]
                s = s + part * part
            sq[rows, :] = s
            x[c, rows, :] = (raw * gain[c].astype(F32)).astype(BF)

        acc_kv[...] += dot(x[c], wkv_b[c])

    mean = jnp.sum(sq[...], axis=1, keepdims=True) * (1.0 / WIDTH)
    rsb[...] = jnp.broadcast_to(lax.rsqrt(mean + EPS), (TOK, HEAD))

    rope_copy.wait()
    start1 = tab[LEN]
    start2 = tab[LEN] + tab[LEN + 1]
    lane = lax.broadcasted_iota(jnp.int32, (TOK, HEAD), 1)
    low = lane < HEAD // 2
    token = me_p * TOK + lax.broadcasted_iota(jnp.int32, (TOK, HEAD), 0)

    def both(row, low_mask):
        turned = pltpu.roll(row, HEAD // 2, 1)
        return jnp.where(low_mask, row, turned), jnp.where(low_mask, turned, row)

    low8 = lax.broadcasted_iota(jnp.int32, (8, HEAD), 1) < HEAD // 2

    def start_row(at):
        return both(jnp.broadcast_to(rope_b[pl.ds(at, 1), :], (8, HEAD)), low8)

    c1, n1 = start_row(start1)
    c2, n2 = start_row(start2)
    tc, tn = both(rope_b[pl.ds(pl.multiple_of(me_p * TOK, TOK), TOK), :], low)
    in1 = token >= start1
    in2 = token >= start2
    sc = jnp.where(in2, c2[0:1, :], jnp.where(in1, c1[0:1, :], 1.0))
    sn = jnp.where(in2, n2[0:1, :], jnp.where(in1, n1[0:1, :], 0.0))
    cosb[...] = tc * sc + tn * sn
    turned = tn * sc - tc * sn
    sinb[...] = jnp.where(low, -turned, turned)

    segment = in1.astype(jnp.int32) + in2.astype(jnp.int32)
    qext[...] = jnp.where((lane < 4) & (lane != segment), MASKED, 0.0).astype(BF)
    row3 = lax.broadcasted_iota(jnp.int32, (HEAD, 3 * TOK), 0)
    ktok = (me_p - 2) * TOK + lax.broadcasted_iota(jnp.int32, (HEAD, 3 * TOK), 1)
    kseg = jnp.where(ktok < 0, 3, (ktok >= start1).astype(jnp.int32) + (ktok >= start2).astype(jnp.int32))
    kext[...] = (row3 == kseg).astype(F32).astype(BF)

    def p2kv(i):
        dp, dg = plane(i)
        return remote(st_kv.at[dg], dkv.at[:, my_rows, my_cols], s2kv.at[i], r2kv_s.at[i], dp, dg, me_t)

    def p2q(i):
        dp, dg = plane(i)
        return remote(st_q.at[dg], dq.at[:, my_rows, my_cols], s2q.at[i], r2q_s.at[i], dp, dg, me_t)

    up_low = pl.ds(pl.multiple_of(me_p * 16, 16), 16)
    up_high = pl.ds(pl.multiple_of(RANK + me_p * 16, 16), 16)

    def p2u(i):
        dp, dg = plane(i)
        return (
            remote(st_u.at[dg, 0], upkv.at[up_low, pl.ds(0, HEAD)], s2u.at[0, i], r2u_s.at[0, i], dp, dg, me_t),
            remote(st_u.at[dg, 1], upkv.at[up_high, pl.ds(HEAD, HEAD)], s2u.at[1, i], r2u_s.at[1, i], dp, dg, me_t),
        )

    own2 = (
        pltpu.make_async_copy(st_kv.at[me_g], dkv.at[:, my_rows, my_cols], loc_sem.at[5]),
        pltpu.make_async_copy(st_u.at[me_g, 0], upkv.at[up_low, pl.ds(0, HEAD)], loc_sem.at[6]),
        pltpu.make_async_copy(st_u.at[me_g, 1], upkv.at[up_high, pl.ds(HEAD, HEAD)], loc_sem.at[7]),
        pltpu.make_async_copy(st_q.at[me_g], dq.at[:, my_rows, my_cols], loc_sem.at[8]),
    )

    def wait_recv_both(pair):
        pair[0].wait_recv()
        pair[1].wait_recv()

    def second_kv():
        for k in range(3):
            own1[k].wait()

        @pl.loop(1, OWNERS)
        def _(i):
            p1kv(i).wait_recv()

        for g in range(GROUP):
            st_kv[g] = r1kv[tab[IDS + g]]

        @pl.loop(1, OWNERS)
        def _(i):
            p2kv(i).start()

        own2[0].start()

        @pl.when(me_g == 0)
        def _():
            @pl.loop(1, OWNERS)
            def _(i):
                wait_recv_both(p1u(i))

            for g in range(GROUP):
                st_u[g] = r1u[tab[IDS + g]]

            @pl.loop(1, OWNERS)
            def _(i):
                start_both(p2u(i))

            own2[1].start()
            own2[2].start()

    def second_q():
        own1[3].wait()
        own1[4].wait()

        @pl.loop(1, OWNERS)
        def _(i):
            wait_recv_both(p1q(i))

        for g in range(GROUP):
            st_q[g] = r1q[tab[IDS + g]]

        @pl.loop(1, OWNERS)
        def _(i):
            p2q(i).start()

        own2[3].start()

    def rs(w, i):
        dt = lax.rem(me_t + i, TENSOR)
        return remote(zst.at[w, dt], zr.at[w, i], srs.at[w, i], rrs.at[w, i], me_p, me_g, dt)

    def ag(w, i):
        dt = lax.rem(me_t + i, TENSOR)
        return remote(zs.at[w], zf.at[w, me_t], sag.at[w, i], rag.at[w, i], me_p, me_g, dt)

    def scatter(w, factors):
        z = dot_t(x[me_t], factors)
        zst[w] = z.astype(BF).reshape(TENSOR, TOK // TENSOR, HEAD)

        @pl.loop(1, TENSOR)
        def _(i):
            rs(w, i).start()

    def gather(w):
        total = zst[w, me_t].astype(F32)
        for i in range(1, TENSOR):
            rs(w, i).wait_recv()
            total = total + zr[w, i].astype(F32)
        summed = total.astype(BF)
        zs[w] = summed
        zf[w, me_t] = summed

        @pl.loop(1, TENSOR)
        def _(i):
            ag(w, i).start()

    def gathered(w):
        @pl.loop(1, TENSOR)
        def _(i):
            ag(w, i).wait_recv()

        return zf[w].reshape(TOK, HEAD)

    def q_tile(j):
        wq_copy(j).wait()
        cols = pl.ds(j * 256, 256)
        acc_q[:, cols] = dot(x[0], wq_b[j, pl.ds(0, CHUNK), :])

        @pl.loop(1, 8)
        def _(c):
            acc_q[:, cols] += dot(x[c], wq_b[j, pl.ds(pl.multiple_of(c * CHUNK, CHUNK), CHUNK), :])

    def rotated(v):
        return v * cosb[...] + pltpu.roll(v, HEAD // 2, 1) * sinb[...]

    second_kv()
    q_tile(0)

    @pl.loop(1, OWNERS)
    def _(i):
        p2kv(i).wait_recv()

    own2[0].wait()
    scatter(0, dkv[...].reshape(2 * RANK, CHUNK))
    second_q()
    q_tile(1)
    gather(0)

    @pl.loop(1, OWNERS)
    def _(i):
        p2q(i).wait_recv()

    own2[3].wait()
    scatter(1, dq[0])
    q_tile(2)

    from_column_zero(lambda i: wait_recv_both(p2u(i)))

    @pl.when(me_g == 0)
    def _():
        own2[1].wait()
        own2[2].wait()

    kv = acc_kv[...] + ADAPTER_SCALE * dot(gathered(0), upkv[...])
    key = rotated(kv[:, :HEAD] * rsb[...] + bias[:, pl.ds(QCOLS, HEAD)].astype(F32))
    value = kv[:, HEAD:] * rsb[...] + bias[:, pl.ds(QCOLS + HEAD, HEAD)].astype(F32)
    kvo[0] = key.astype(BF).reshape(TOK // PAGE, PAGE, HEAD)
    kvo[1] = value.astype(BF).reshape(TOK // PAGE, PAGE, HEAD)

    def ahead(step):
        return remote(kvo, kvp.at[2 - step], skv.at[step], rkv.at[step], me_p + step, me_g, me_t)

    @pl.when(me_p < POOL - 1)
    def _():
        ahead(1).start()

    @pl.when(me_p < POOL - 2)
    def _():
        ahead(2).start()

    def page_copy(i):
        dp, dg = plane(i)
        dest = dp * GROUP + dg
        return remote(pst.at[pl.ds(dest * 2, 2)], prv.at[mine2], spg.at[i], rpg.at[i], dp, dg, me_t)

    @pl.loop(0, 2 * OWNERS)
    def _(n):
        page = tab[SEND + n]
        pst[n, 0] = kvo[0, page]
        pst[n, 1] = kvo[1, page]

    @pl.loop(1, OWNERS)
    def _(i):
        page_copy(i).start()

    prv[mine2] = pst[mine2]

    gather(1)
    q_tile(3)

    zq = gathered(1)
    for j in range(4):
        cols = pl.ds(j * 256, 256)
        q = acc_q[:, cols] + ADAPTER_SCALE * dot(zq, dq[1, :, cols])
        for h in range(2):
            head = q[:, h * HEAD : (h + 1) * HEAD] * rsb[...] + bias[:, pl.ds(j * 256 + h * HEAD, HEAD)].astype(F32)
            qbuf[2 * j + h] = (rotated(head) * (HEAD**-0.5 * math.log2(math.e))).astype(BF)

    @pl.when(me_p >= 1)
    def _():
        ahead(1).wait_recv()

    @pl.when(me_p >= 2)
    def _():
        ahead(2).wait_recv()

    blocks = (kvp.at[0], kvp.at[1], kvo)
    for s in range(3):
        kt[:, pl.ds(s * TOK, TOK)] = blocks[s][0].reshape(TOK, HEAD).T

    ones = jnp.ones((KWIN, HEAD), BF)
    causal = lax.broadcasted_iota(jnp.int32, (QB, QB), 0) >= lax.broadcasted_iota(jnp.int32, (QB, QB), 1)

    for b in range(TOK // QB):
        rows = pl.ds(b * QB, QB)
        keys = jnp.concatenate([kt[:, pl.ds(b * QB, KWIN)], kext[:, pl.ds(b * QB, KWIN)]], axis=0)
        parts = [blocks[s][1].reshape(TOK, HEAD) for s in range(3)]
        values = jnp.concatenate(parts, axis=0)[b * QB : b * QB + KWIN]
        values = jnp.concatenate([values, ones], axis=1)

        @pl.loop(0, HEADS)
        def _(h):
            query = jnp.concatenate([qbuf[h, rows, :], qext[rows, :]], axis=1)
            score = dot(query, keys)
            last = jnp.where(causal, score[:, KWIN - QB :], MASKED)
            score = jnp.concatenate([score[:, : KWIN - QB], last], axis=1)
            top = jnp.max(score, axis=1, keepdims=True)
            weight = jnp.exp2(score - top).astype(BF)
            total = dot(weight, values)
            out[0, rows, pl.ds(pl.multiple_of(h * HEAD, HEAD), HEAD)] = (total[:, :HEAD] / total[:, HEAD:]).astype(BF)

    @pl.loop(1, OWNERS)
    def _(i):
        page_copy(i).wait_recv()

    @pl.loop(0, 2 * OWNERS)
    def _(n):
        store[n, 0] = prv[tab[RECV + n]]

    @pl.loop(1, OWNERS)
    def _(i):
        p1kv(i).wait_send()
        for cp in p1q(i):
            cp.wait_send()
        p2kv(i).wait_send()
        p2q(i).wait_send()
        page_copy(i).wait_send()

    def sent(pair):
        pair[0].wait_send()
        pair[1].wait_send()

    to_column_zero(lambda i: sent(p1u(i)))

    @pl.when(me_g == 0)
    def _():
        @pl.loop(1, OWNERS)
        def _(i):
            sent(p2u(i))

    @pl.loop(1, TENSOR)
    def _(i):
        for w in range(2):
            rs(w, i).wait_send()
            ag(w, i).wait_send()

    @pl.when(me_p < POOL - 1)
    def _():
        ahead(1).wait_send()

    @pl.when(me_p < POOL - 2)
    def _():
        ahead(2).wait_send()


def rope_table():
    positions = np.arange(2048, dtype=np.float64)[:, None]
    frequency = ROPE_THETA ** (-np.arange(64, dtype=np.float64) * 2.0 / HEAD)
    angle = positions * frequency[None, :]
    return np.concatenate([np.cos(angle), np.sin(angle)], axis=1).astype(np.float32)


def page_lists(table, me_p, me_g):
    owner = me_p * GROUP + me_g
    mine = lax.dynamic_slice_in_dim(table, me_g * 128 + me_p * 32, 32)
    number = jnp.arange(32, dtype=jnp.int32)
    order = jnp.sum((mine[None, :] < mine[:, None]).astype(jnp.int32), axis=1)
    send = jnp.sum(jnp.where(order[None, :] == number[:, None], number[None, :], 0), axis=1)
    slots = owner * 32 + number
    pages = jnp.arange(512, dtype=jnp.int32)
    sources = (pages % 128) // 32 * GROUP + pages // 128
    source = jnp.sum(jnp.where(table[None, :] == slots[:, None], sources[None, :], 0), axis=1)
    earlier = (source[None, :] == source[:, None]) & (number[None, :] < number[:, None])
    recv = source * 2 + jnp.sum(earlier.astype(jnp.int32), axis=1)
    return send, recv


def per_device(
    tokens, gain, wq, wk, wv, bq, bk, bv, down, upq, upk, upv, ids, lengths, table
):
    send, recv = page_lists(table, lax.axis_index("pool"), lax.axis_index("group"))
    tab = jnp.concatenate([ids, lengths[0], jnp.zeros((1,), jnp.int32), send, recv]).astype(jnp.int32)
    bias = jnp.concatenate([bq, bk, bv]).reshape(1, QCOLS + 2 * HEAD)
    smem = pl.BlockSpec(memory_space=pltpu.SMEM)
    vmem = pl.BlockSpec(memory_space=pltpu.VMEM)
    hbm = pl.BlockSpec(memory_space=pl.ANY)
    V = pltpu.VMEM
    D = pltpu.SemaphoreType.DMA
    scratch = [
        V((8, TOK, CHUNK), BF),
        V((8, CHUNK, 256), BF),
        V((4, WIDTH, 256), BF),
        V((TOK, 256), F32),
        V((TOK, QCOLS), F32),
        V((TOK, HEAD), F32),
        V((TOK, HEAD), F32),
        V((2048, HEAD), F32),
        V((TOK, HEAD), F32),
        V((TOK, HEAD), F32),
        V((32, 2, 16, 256), BF),
        V((32, 2, 16, HEAD), BF),
        V((32, 2, 16, 256), BF),
        V((4, 2, 16, 256), BF),
        V((4, 2, 16, HEAD), BF),
        V((4, 2, 16, 256), BF),
        V((2, RANK, CHUNK), BF),
        V((2 * RANK, 256), BF),
        V((2, 2 * RANK, CHUNK), BF),
        V((2, 8, 64, HEAD), BF),
        V((2, 8, 64, HEAD), BF),
        V((2, 64, HEAD), BF),
        V((2, 8, 64, HEAD), BF),
        V((2, 32, PAGE, HEAD), BF),
        V((2, 2, 32, PAGE, HEAD), BF),
        V((32, 2, PAGE, HEAD), BF),
        V((32, 2, PAGE, HEAD), BF),
        V((HEADS, TOK, HEAD), BF),
        V((TOK, HEAD), BF),
        V((HEAD, 3 * TOK), BF),
        V((HEAD, 3 * TOK), BF),
        D((8,)), D((8, 2)), D((4,)), D, D((9,)),
        D((16,)), D((2, 16)), D((2, 16)), D((16,)), D((2, 16)), D((16,)), D((2, 8)), D((2, 8)), D((3,)), D((16,)),
        D((16,)), D((2, 16)), D((2, 16)), D((16,)), D((2, 16)), D((16,)), D((2, 8)), D((2, 8)), D((3,)), D((16,)),
    ]
    return pl.pallas_call(
        kernel,
        out_shape=(
            jax.ShapeDtypeStruct((1, TOK, QCOLS), BF),
            jax.ShapeDtypeStruct((32, 1, 2, PAGE, HEAD), BF),
        ),
        in_specs=[smem, hbm, vmem, hbm, hbm, hbm, vmem, hbm, hbm, hbm, hbm, hbm],
        out_specs=(vmem, vmem),
        scratch_shapes=scratch,
        compiler_params=pltpu.CompilerParams(
            collective_id=0, has_side_effects=True, vmem_limit_bytes=60 * 1024 * 1024
        ),
        name="layer",
    )(tab, tokens, gain.reshape(8, 1, CHUNK), wq, wk, wv, bias, down, upq, upk, upv, jnp.asarray(rope_table()))


def solution(mesh):
    placed = (
        P("group", "pool", None),
        P(),
        P(None, "tensor"),
        P(None, "tensor"),
        P(None, "tensor"),
        P("tensor"),
        P("tensor"),
        P("tensor"),
        P(("pool", "group"), None, None, "tensor"),
        P(("pool", "group"), None, "tensor"),
        P(("pool", "group"), None, "tensor"),
        P(("pool", "group"), None, "tensor"),
        P(),
        P("group", None),
        P(),
    )
    return jax.shard_map(
        per_device,
        mesh=mesh,
        in_specs=placed,
        out_specs=(P("group", "pool", "tensor"), P(("pool", "group"), "tensor", None, None, None)),
        check_vma=False,
    )
```

time: 276 us -> 85.1 us (0.31); the launches traced: 272 us -> 84.7 us
  waiting for transfers between devices: 91.4 us -> 0 us
  Pallas kernels: 0 us -> 74 us
  matrix products: 64.1 us -> 0 us
  local copies, waits for them, and re-layouts: 39.1 us -> 7.93 us
  other arithmetic: 29.8 us -> 2.08 us
  blocking collectives: 26.5 us -> 0 us
  between operations: 14.4 us -> 0.67 us
  starting transfers between devices: 6.9 us -> 0 us
    psum x1 -> x0, waiting for transfers between devices: 91.3 us -> none  [per_device(): lax.psum(contributions[0], ('pool', 'group')).astype(jnp.float32)]
    pallas_call x0 -> x1, Pallas kernels: none -> 74 us  [per_device(): pl.pallas_call(kernel, out_shape=(jax.ShapeDtypeStruct((1, TOK, QCOLS), B...]
    dot_general x12 -> x0, matrix products: 64.1 us -> none  [the longest x3 17.8 us: per_device(): jnp.dot(shard_part[group_member].T, up_factor, preferred_element_type=jnp...]
    unnamed x30 -> x2, local copies, waits for them, and re-layouts: 36.3 us -> 3.93 us
    all_gather x2 -> x0, blocking collectives: 26.5 us -> none  [the longest x1 13.4 us: per_device(): value_piece = lax.all_gather(value_row_block, 'pool', axis=0, tiled=True)]
    reduce_sum x5 -> x4, other arithmetic: 20.2 us -> 1.34 us  [the longest x1 0.86 us: page_lists(): jnp.sum(jnp.where(table[None, :] == slots[:, None], sources[None, :], 0),...]
    all_to_all x1 -> x0, starting transfers between devices: 6.64 us -> none  [per_device(): lax.all_to_all(outgoing, ('pool', 'group'), split_axis=0, concat_axis=0,...]
  transfers between devices with their start and end apart: 3 -> 0, of which waited for: 1 -> 0; matrix products, arithmetic and copies ran while one was open for 31% -> 0% of each run, Pallas kernels for 0% -> 0%
where the time goes in v1:
time: 85.1 us; the launch traced here: 84.7 us
  Pallas kernels  74 us (87%)
  local copies, waits for them, and re-layouts  7.93 us (9%)
  other arithmetic  2.08 us (2%)
    pallas_call x1, Pallas kernels, per_device(): pl.pallas_call(kernel, out_shape=(jax.ShapeDtypeStruct((1, TOK, QCOLS), B...  74 us
    unnamed x2, local copies, waits for them, and re-layouts  3.93 us

profile of v1, /device:TPU:64, one launch (start us, length us, event | category | flops | bytes accessed | tf_op | source)
XLA Modules:
  0.0 84.7 jit_solution(11024379545268763917)
XLA Ops:
  0.6 0.8 dynamic_slice.3
  1.4 0.2 convert_reduce_fusion.1
  1.6 0.1 select_reduce_fusion.1
  1.7 0.9 %select_reduce_fusion = s32[32]{0:T(128)S(1)} fusion(s32[512]{0:T(512)S(1)} %fusion.7, s32[512]{0:T(512)} %param.30, s32[32]{0:T(128)S(1)} %iota_add_fusion), kind=kLoop, calls=%fused_computation | loop fusion | flops 49120 | bytes 4352 | tf_op jit(solution)/shard_map/reduce_sum | solution.py:548
  2.6 0.2 convert_reduce_fusion
  2.8 1.3 %concatenate.6.tab = s32[72]{0:T(128)} concatenate(s32[4]{0:T(128)} %param.28, s32[3]{0:T(128)} %bitcast.1, s32[1]{0:T(128)} %constant.49.clone.1, s32[32]{0:T(128)S(1)} %select_reduce_fusion.1, s32[32]{0:T(128)S(1)} %multiply_add_fusion), dimensions={0} | concatenate | bytes 576 | tf_op jit(solution)/shard_map/concatenate | solution.py:558
  4.1 0.7 pad_maximum_fusion
  4.8 0.6 reshape.58.bias
  5.4 1.3 %reshape.59.gain = bf16[8,1,1024]{2,1,0:T(2,128)(2,1)} reshape(bf16[8192]{0:T(1024)(128)(2,1)} %param.17) | data formatting | bytes 32768 | tf_op jit(solution)/shard_map/reshape | solution.py:614
  6.8 74.0 %layer.1 = (bf16[1,512,1024]{2,1,0:T(8,128)(2,1)}, bf16[32,1,2,16,128]{4,3,2,1,0:T(8,128)(2,1)}) custom-call(s32[72]{0:T(128)} %concatenate.6.tab, bf16[1,512,8192]{2,1,0:T(8,128)(2,1)} %tokens.1, bf16[8,1,1024]{2,1,0:T(2,128)(2,1)} %reshape.59.gain, bf16[8192,1024]{1,0:T(8,128)(2,1)} %wq.1, bf16[8192,128]{1,0:T(8,128)(2,1)} %wk.1, bf16[8192,128]{1,0:T(8,128)(2,1)} %wv.1, ...), custom_call_target="tpu_custom_call" | custom-call | tf_op jit(solution)/shard_map/layer/pallas_call | solution.py:601
  80.8 2.3 %copy.22 = bf16[1,512,1024]{2,1,0:T(8,128)(2,1)} copy(bf16[1,512,1024]{2,1,0:T(8,128)(2,1)} %get-tuple-element.4) | data formatting | bytes 2097152
  83.0 1.7 %copy.23 = bf16[32,1,2,16,128]{4,3,2,1,0:T(8,128)(2,1)} copy(bf16[32,1,2,16,128]{4,3,2,1,0:T(8,128)(2,1)} %get-tuple-element.5) | data formatting | bytes 524288
  (3 shorter events, 0.0 us)

commit v2 on v1

v2 whole, which is shorter than its diff:
```python
import functools
import math

import jax
import jax.numpy as jnp
import numpy as np
from jax import lax
from jax.experimental import pallas as pl
from jax.experimental.pallas import tpu as pltpu
from jax.sharding import PartitionSpec as P

HEAD = 128
PAGE = 16
RANK = 64
ADAPTER_SCALE = 2.0
ROPE_THETA = 1000000.0
EPS = 1e-06
MASKED = -1e30
BF = jnp.bfloat16
F32 = jnp.float32
MESH = pl.DeviceIdType.MESH
POOL = 4
GROUP = 4
OWNERS = 16
TENSOR = 8
TOK = 512
WIDTH = 8192
CHUNK = 1024
QCOLS = 1024
HEADS = 8
QB = 256
KWIN = 1280


def dot(a, b):
    return jnp.dot(a, b, preferred_element_type=F32)


def dot_t(a, b):
    return lax.dot_general(a, b, (((1,), (1,)), ((), ())), preferred_element_type=F32)


def kernel(
    ids, lengths, lists, tokens, vec, wq, wk, wv, down, upq, upk, upv, rope,
    out, store,
    x, wkv_b, wq_b, acc_kv, acc_q, sq, rsb, vecb, rope_b, cosb, sinb,
    r1, r1u, st, stu, fac, upkv, zst, zr, zs, zf,
    kvo, kvp, pst, prv, qx, kx, vx, top_b, sum_b,
    tok_sem, wkv_sem, wq_sem, misc, own_u,
    s1, s1u, s2, s2u, srs, sag, skv, spg,
    v1, v1u, v2, v2u, vrs, vag, vkv, vpg,
):
    me_p = lax.axis_index("pool")
    me_g = lax.axis_index("group")
    me_t = lax.axis_index("tensor")
    owner = me_p * GROUP + me_g

    def chunk(c):
        return pl.ds(pl.multiple_of(c * CHUNK, CHUNK), CHUNK)

    def tok_copy(c):
        return pltpu.make_async_copy(tokens.at[0, :, chunk(c)], x.at[c], tok_sem.at[c])

    def wkv_start(c):
        for n, src in enumerate((wk, wv)):
            pltpu.make_async_copy(src.at[chunk(c), :], wkv_b.at[c, :, pl.ds(n * HEAD, HEAD)], wkv_sem.at[c]).start()

    def arrived(ref, sem):
        pltpu.make_async_copy(ref, ref, sem).wait()

    def wq_copy(j):
        return pltpu.make_async_copy(wq.at[:, pl.ds(j * 256, 256)], wq_b.at[j], wq_sem.at[j])

    vec_copy = pltpu.make_async_copy(vec, vecb, misc.at[0])
    rope_copy = pltpu.make_async_copy(rope, rope_b, misc.at[1])

    upkv[...] = jnp.zeros_like(upkv)

    barrier = pltpu.get_barrier_semaphore()

    def plane(i):
        dest = lax.rem(owner + i, OWNERS)
        return dest // GROUP, lax.rem(dest, GROUP)

    def around(i):
        return lax.rem(me_t + i, TENSOR)

    @pl.loop(1, OWNERS)
    def _(i):
        dp, dg = plane(i)
        pl.semaphore_signal(barrier, inc=1, device_id=(dp, dg, me_t), device_id_type=MESH)

    @pl.loop(1, TENSOR)
    def _(i):
        pl.semaphore_signal(barrier, inc=1, device_id=(me_p, me_g, around(i)), device_id_type=MESH)

    vec_copy.start()
    for c in range(2):
        tok_copy(c).start()
        wkv_start(c)

    pl.semaphore_wait(barrier, OWNERS - 1 + TENSOR - 1)

    mine2 = pl.ds(owner * 2, 2)

    def rows_of(dp):
        return pl.ds(pl.multiple_of(dp * 16, 16), 16)

    def cols_of(dg):
        return pl.ds(pl.multiple_of(dg * 256, 256), 256)

    def remote(src, dst, send, recv, dp, dg, dt):
        return pltpu.make_async_remote_copy(
            src_ref=src, dst_ref=dst, send_sem=send, recv_sem=recv,
            device_id=(dp, dg, dt), device_id_type=MESH,
        )

    @pl.loop(1, OWNERS)
    def _(i):
        dp, dg = plane(i)
        rows, cols = rows_of(dp), cols_of(dg)
        remote(down.at[:, :, rows, cols], r1.at[mine2, pl.ds(0, 3)], s1, v1, dp, dg, me_t).start()
        remote(upq.at[:, rows, cols], r1.at[mine2, 3], s1, v1, dp, dg, me_t).start()

    pltpu.make_async_copy(down.at[:, :, rows_of(me_p), cols_of(me_g)], r1.at[mine2, pl.ds(0, 3)], v1).start()
    pltpu.make_async_copy(upq.at[:, rows_of(me_p), cols_of(me_g)], r1.at[mine2, 3], v1).start()

    for n, src in enumerate((upk, upv)):
        for dp in range(POOL):
            dest = dp * GROUP + n

            @pl.when(dest != owner)
            def _():
                remote(src.at[:, pl.ds(dp * 16, 16), :], r1u.at[mine2], s1u, v1u, dp, n, me_t).start()

        @pl.when(me_g == n)
        def _():
            pltpu.make_async_copy(src.at[:, rows_of(me_p), :], r1u.at[mine2], v1u).start()

    for c in range(2, 8):
        tok_copy(c).start()
        wkv_start(c)
    rope_copy.start()
    for j in range(4):
        wq_copy(j).start()

    sq[...] = jnp.zeros_like(sq)
    acc_kv[...] = jnp.zeros_like(acc_kv)
    vec_copy.wait()

    @pl.loop(0, 8)
    def _(c):
        tok_copy(c).wait()

        @pl.loop(0, TOK // 64)
        def _(r):
            rows = pl.ds(pl.multiple_of(r * 64, 64), 64)
            s = sq[rows, :]
            for k in range(CHUNK // 128):
                lanes = pl.ds(k * 128, 128)
                part = x[c, rows, lanes].astype(F32)
                s = s + part * part
                x[c, rows, lanes] = (part * vecb[pl.ds(c * 8 + k, 1), :]).astype(BF)
            sq[rows, :] = s

        arrived(wkv_b.at[c], wkv_sem.at[c])
        acc_kv[...] += dot(x[c], wkv_b[c])

    mean = jnp.sum(sq[...], axis=1, keepdims=True) * (1.0 / WIDTH)
    rsb[...] = jnp.broadcast_to(lax.rsqrt(mean + EPS), (TOK, HEAD))

    def q_tile(j):
        wq_copy(j).wait()
        cols = pl.ds(j * 256, 256)
        acc_q[:, cols] = dot(x[0], wq_b[j, pl.ds(0, CHUNK), :])

        @pl.loop(1, 8)
        def _(c):
            acc_q[:, cols] += dot(x[c], wq_b[j, chunk(c), :])

    q_tile(0)
    q_tile(1)
    q_tile(2)

    arrived(r1, v1)
    for g in range(GROUP):
        st[g] = r1[ids[g]]

    @pl.loop(1, OWNERS)
    def _(i):
        dp, dg = plane(i)
        remote(st.at[dg], fac.at[:, rows_of(me_p), cols_of(me_g)], s2, v2, dp, dg, me_t).start()

    pltpu.make_async_copy(st.at[me_g], fac.at[:, rows_of(me_p), cols_of(me_g)], v2).start()

    def up_place(n):
        first = RANK * (n + 1) + me_p * 16
        return upkv.at[pl.ds(pl.multiple_of(first, 16), 16), pl.ds(n * HEAD, HEAD)]

    for n in range(2):

        @pl.when(me_g == n)
        def _():
            arrived(r1u, v1u)
            for g in range(GROUP):
                stu[g] = r1u[ids[g]]

            @pl.loop(1, OWNERS)
            def _(i):
                dp, dg = plane(i)
                remote(stu.at[dg], up_place(n), s2u, v2u.at[n], dp, dg, me_t).start()

            pltpu.make_async_copy(stu.at[me_g], up_place(n), v2u.at[n]).start()

    rope_copy.wait()
    start1 = lengths[0, 0]
    start2 = lengths[0, 0] + lengths[0, 1]
    lane = lax.broadcasted_iota(jnp.int32, (TOK, HEAD), 1)
    low = lane < HEAD // 2
    token = me_p * TOK + lax.broadcasted_iota(jnp.int32, (TOK, HEAD), 0)

    def both(row, low_mask):
        turned = pltpu.roll(row, HEAD // 2, 1)
        return jnp.where(low_mask, row, turned), jnp.where(low_mask, turned, row)

    low8 = lax.broadcasted_iota(jnp.int32, (8, HEAD), 1) < HEAD // 2

    def start_row(at):
        return both(jnp.broadcast_to(rope_b[pl.ds(at, 1), :], (8, HEAD)), low8)

    c1, n1 = start_row(start1)
    c2, n2 = start_row(start2)
    tc, tn = both(rope_b[pl.ds(pl.multiple_of(me_p * TOK, TOK), TOK), :], low)
    in1 = token >= start1
    in2 = token >= start2
    sc = jnp.where(in2, c2[0:1, :], jnp.where(in1, c1[0:1, :], 1.0))
    sn = jnp.where(in2, n2[0:1, :], jnp.where(in1, n1[0:1, :], 0.0))
    cosb[...] = tc * sc + tn * sn
    swung = tn * sc - tc * sn
    sinb[...] = jnp.where(low, -swung, swung)

    segment = in1.astype(jnp.int32) + in2.astype(jnp.int32)
    marks = jnp.where((lane < 4) & (lane != segment), MASKED, 0.0).astype(BF)
    for h in range(HEADS):
        qx[h, :, pl.ds(HEAD, HEAD)] = marks
    mark_row = lax.broadcasted_iota(jnp.int32, (HEAD, 3 * TOK), 0)
    ktok = (me_p - 2) * TOK + lax.broadcasted_iota(jnp.int32, (HEAD, 3 * TOK), 1)
    kseg = (ktok >= start1).astype(jnp.int32) + (ktok >= start2).astype(jnp.int32)
    kx[pl.ds(HEAD, HEAD), :] = (mark_row == kseg).astype(F32).astype(BF)
    for n in range(3):
        vx[n, :, pl.ds(HEAD, HEAD)] = jnp.ones((TOK, HEAD), BF)

    arrived(fac, v2)
    z = dot_t(x[me_t], fac[...].reshape(4 * RANK, CHUNK))
    zst[...] = z.astype(BF).reshape(TENSOR, TOK // TENSOR, 4 * RANK)

    @pl.loop(1, TENSOR)
    def _(i):
        dt = around(i)
        remote(zst.at[dt], zr.at[i - 1], srs, vrs, me_p, me_g, dt).start()

    q_tile(3)
    arrived(zr, vrs)
    total = zst[me_t].astype(F32)
    for i in range(TENSOR - 1):
        total = total + zr[i].astype(F32)
    zs[...] = total.astype(BF)

    @pl.loop(1, TENSOR)
    def _(i):
        remote(zs, zf.at[me_t], sag, vag, me_p, me_g, around(i)).start()

    pltpu.make_async_copy(zs, zf.at[me_t], vag).start()
    for n in range(2):
        arrived(upkv.at[pl.ds(RANK * (n + 1), RANK), pl.ds(n * HEAD, HEAD)], v2u.at[n])
    arrived(zf, vag)
    low_rank = zf[...].reshape(TOK, 4 * RANK)

    def rotated(v):
        return v * cosb[...] + pltpu.roll(v, HEAD // 2, 1) * sinb[...]

    def bias(n):
        return vecb[pl.ds(64 + n, 1), :]

    kv = acc_kv[...] + ADAPTER_SCALE * dot(low_rank, upkv[...])
    key = rotated(kv[:, :HEAD] * rsb[...] + bias(8)).astype(BF)
    value = (kv[:, HEAD:] * rsb[...] + bias(9)).astype(BF)
    kvo[0] = key.reshape(TOK // PAGE, PAGE, HEAD)
    kvo[1] = value.reshape(TOK // PAGE, PAGE, HEAD)

    def ahead(step):
        return remote(kvo, kvp.at[2 - step], skv.at[step - 1], vkv.at[step - 1], me_p + step, me_g, me_t)

    for step in (1, 2):

        @pl.when(me_p < POOL - step)
        def _():
            ahead(step).start()

    @pl.loop(0, 2 * OWNERS)
    def _(n):
        page = lists[0, me_g * POOL + me_p, n]
        pst[n, 0] = kvo[0, page]
        pst[n, 1] = kvo[1, page]

    @pl.loop(1, OWNERS)
    def _(i):
        dp, dg = plane(i)
        dest = dp * GROUP + dg
        remote(pst.at[pl.ds(dest * 2, 2)], prv.at[mine2], spg, vpg, dp, dg, me_t).start()

    pltpu.make_async_copy(pst.at[mine2], prv.at[mine2], vpg).start()

    for j in range(4):
        q = acc_q[:, pl.ds(j * 256, 256)] + ADAPTER_SCALE * dot(low_rank[:, :RANK], fac[3, :, pl.ds(j * 256, 256)])
        for h in range(2):
            head = q[:, h * HEAD : (h + 1) * HEAD] * rsb[...] + bias(2 * j + h)
            qx[2 * j + h, :, pl.ds(0, HEAD)] = (rotated(head) * (HEAD**-0.5 * math.log2(math.e))).astype(BF)

    def place(n, ref):
        kx[pl.ds(0, HEAD), pl.ds(n * TOK, TOK)] = ref[0].reshape(TOK, HEAD).T
        vx[n, :, pl.ds(0, HEAD)] = ref[1].reshape(TOK, HEAD)

    causal = lax.broadcasted_iota(jnp.int32, (QB, QB), 0) >= lax.broadcasted_iota(jnp.int32, (QB, QB), 1)

    def attend(h, rows, n, first, count, diagonal):
        score = dot(qx[h, rows, :], kx[:, pl.ds(n * TOK + first, count)])
        if diagonal:
            last = jnp.where(causal, score[:, count - QB :], MASKED)
            score = last if count == QB else jnp.concatenate([score[:, : count - QB], last], axis=1)
        top = jnp.max(score, axis=1, keepdims=True)
        if not diagonal:
            before = top_b[h, rows, :]
            top = jnp.maximum(before[:, :1], top)
        weight = jnp.exp2(score - top).astype(BF)
        part = dot(weight, vx[n, pl.ds(first, count), :])
        wide = jnp.broadcast_to(top, (top.shape[0], HEAD))
        if not diagonal:
            fade = jnp.exp2(before - wide)
            part = part + sum_b[h, rows, :] * jnp.concatenate([fade, fade], axis=1)
        sum_b[h, rows, :] = part
        top_b[h, rows, :] = wide

    upper, lower, every = pl.ds(0, QB), pl.ds(QB, QB), pl.ds(0, TOK)
    place(2, kvo)

    @pl.loop(0, HEADS)
    def _(h):
        attend(h, upper, 2, 0, QB, True)
        attend(h, lower, 2, 0, TOK, True)

    @pl.when(me_p >= 1)
    def _():
        ahead(1).wait_recv()
        place(1, kvp.at[1])

        @pl.loop(0, HEADS)
        def _(h):
            attend(h, every, 1, 0, TOK, False)

    @pl.when(me_p >= 2)
    def _():
        ahead(2).wait_recv()
        place(0, kvp.at[0])

        @pl.loop(0, HEADS)
        def _(h):
            attend(h, upper, 0, 0, TOK, False)
            attend(h, lower, 0, QB, QB, False)

    @pl.loop(0, HEADS)
    def _(h):
        both_parts = sum_b[h]
        out[0, :, pl.ds(pl.multiple_of(h * HEAD, HEAD), HEAD)] = (both_parts[:, :HEAD] / both_parts[:, HEAD:]).astype(BF)

    arrived(prv, vpg)

    @pl.loop(0, 2 * OWNERS)
    def _(n):
        store[n, 0] = prv[lists[1, owner, n]]

    arrived(r1.at[pl.ds(0, 2 * (OWNERS - 1))], s1)
    arrived(r1.at[pl.ds(0, OWNERS - 1)], s2)
    arrived(zr, srs)
    arrived(zr, sag)
    arrived(prv.at[pl.ds(0, 2 * (OWNERS - 1))], spg)

    @pl.when(me_g < 2)
    def _():
        arrived(r1u.at[pl.ds(0, 2 * 7)], s1u)
        arrived(r1u.at[pl.ds(0, OWNERS - 1)], s2u)

    @pl.when(me_g >= 2)
    def _():
        arrived(r1u.at[pl.ds(0, 2 * 8)], s1u)

    for step in (1, 2):

        @pl.when(me_p < POOL - step)
        def _():
            ahead(step).wait_send()


def rope_table():
    positions = np.arange(2048, dtype=np.float64)[:, None]
    frequency = ROPE_THETA ** (-np.arange(64, dtype=np.float64) * 2.0 / HEAD)
    angle = positions * frequency[None, :]
    return np.concatenate([np.cos(angle), np.sin(angle)], axis=1).astype(np.float32)


def page_lists(table):
    slots = table.reshape(16, 32)
    number = jnp.arange(32, dtype=jnp.int32)
    order = jnp.sum((slots[:, None, :] < slots[:, :, None]).astype(jnp.int32), axis=2)
    send = jnp.sum(jnp.where(order[:, None, :] == number[None, :, None], number[None, None, :], 0), axis=2)
    pages = jnp.arange(512, dtype=jnp.int32)
    sources = (pages % 128) // 32 * GROUP + pages // 128
    wanted = pages.reshape(16, 32)
    source = jnp.sum(jnp.where(table[None, None, :] == wanted[:, :, None], sources[None, None, :], 0), axis=2)
    earlier = (source[:, None, :] == source[:, :, None]) & (number[None, None, :] < number[None, :, None])
    recv = source * 2 + jnp.sum(earlier.astype(jnp.int32), axis=2)
    return jnp.stack([send, recv])


def per_device(
    tokens, gain, wq, wk, wv, bq, bk, bv, down, upq, upk, upv, ids, lengths, table
):
    vec = jnp.concatenate([gain, bq, bk, bv]).astype(F32).reshape(74, HEAD)
    smem = pl.BlockSpec(memory_space=pltpu.SMEM)
    vmem = pl.BlockSpec(memory_space=pltpu.VMEM)
    hbm = pl.BlockSpec(memory_space=pl.ANY)
    V = pltpu.VMEM
    D = pltpu.SemaphoreType.DMA
    scratch = [
        V((8, TOK, CHUNK), BF),
        V((8, CHUNK, 256), BF),
        V((4, WIDTH, 256), BF),
        V((TOK, 256), F32),
        V((TOK, QCOLS), F32),
        V((TOK, HEAD), F32),
        V((TOK, HEAD), F32),
        V((74, HEAD), F32),
        V((2048, HEAD), F32),
        V((TOK, HEAD), F32),
        V((TOK, HEAD), F32),
        V((32, 4, 16, 256), BF),
        V((32, 16, HEAD), BF),
        V((4, 4, 16, 256), BF),
        V((4, 16, HEAD), BF),
        V((4, RANK, CHUNK), BF),
        V((4 * RANK, 256), BF),
        V((8, 64, 256), BF),
        V((7, 64, 256), BF),
        V((64, 256), BF),
        V((8, 64, 256), BF),
        V((2, 32, PAGE, HEAD), BF),
        V((2, 2, 32, PAGE, HEAD), BF),
        V((32, 2, PAGE, HEAD), BF),
        V((32, 2, PAGE, HEAD), BF),
        V((HEADS, TOK, 2 * HEAD), BF),
        V((2 * HEAD, 3 * TOK), BF),
        V((3, TOK, 2 * HEAD), BF),
        V((HEADS, TOK, HEAD), F32),
        V((HEADS, TOK, 2 * HEAD), F32),
        D((8,)), D((8,)), D((4,)), D((2,)), D,
        D, D, D, D, D, D, D((2,)), D,
        D, D, D, D((2,)), D, D, D((2,)), D,
    ]
    return pl.pallas_call(
        kernel,
        out_shape=(
            jax.ShapeDtypeStruct((1, TOK, QCOLS), BF),
            jax.ShapeDtypeStruct((32, 1, 2, PAGE, HEAD), BF),
        ),
        in_specs=[smem, smem, smem] + [hbm] * 10,
        out_specs=(vmem, vmem),
        scratch_shapes=scratch,
        compiler_params=pltpu.CompilerParams(
            collective_id=0, has_side_effects=True, vmem_limit_bytes=60 * 1024 * 1024
        ),
        name="layer",
    )(ids, lengths, page_lists(table), tokens, vec, wq, wk, wv, down, upq, upk, upv, jnp.asarray(rope_table()))


def solution(mesh):
    placed = (
        P("group", "pool", None),
        P(),
        P(None, "tensor"),
        P(None, "tensor"),
        P(None, "tensor"),
        P("tensor"),
        P("tensor"),
        P("tensor"),
        P(("pool", "group"), None, None, "tensor"),
        P(("pool", "group"), None, "tensor"),
        P(("pool", "group"), None, "tensor"),
        P(("pool", "group"), None, "tensor"),
        P(),
        P("group", None),
        P(),
    )
    return jax.shard_map(
        per_device,
        mesh=mesh,
        in_specs=placed,
        out_specs=(P("group", "pool", "tensor"), P(("pool", "group"), "tensor", None, None, None)),
        check_vma=False,
    )
```

time: 85.1 us -> 82.6 us (0.971)
  local copies, waits for them, and re-layouts: 7.93 us -> 4.69 us
  other arithmetic: 2.08 us -> 4.44 us
  Pallas kernels: 74 us -> 72.4 us
    reshape x2 -> x0, local copies, waits for them, and re-layouts: 1.94 us -> none  [the longest x1 1.34 us: per_device(): gain.reshape(8, 1, CHUNK)]
    pallas_call x1, Pallas kernels: 74 us -> 72.4 us  [per_device(): pl.pallas_call(kernel, out_shape=(jax.ShapeDtypeStruct((1, TOK, QCOLS), B...]
    convert_element_type x0 -> x1, other arithmetic: none -> 1.39 us  [per_device(): vec = jnp.concatenate([gain, bq, bk, bv]).astype(F32).reshape(74, HEAD)]
    concatenate x1 -> x0, local copies, waits for them, and re-layouts: 1.3 us -> none  [per_device(): jnp.concatenate([ids, lengths[0], jnp.zeros((1,), jnp.int32), send, recv])]
    reduce_sum x4, other arithmetic: 1.34 us -> 2.41 us  [the longest x1 1.15 us: page_lists(): jnp.sum(jnp.where(table[None, None, :] == wanted[:, :, None], sources[Non...]
where the time goes in v2:
time: 82.6 us; the launch traced here: 82.2 us
  Pallas kernels  72.4 us (88%)
  local copies, waits for them, and re-layouts  4.69 us (6%)
  other arithmetic  4.44 us (5%)
    pallas_call x1, Pallas kernels, per_device(): pl.pallas_call(kernel, out_shape=(jax.ShapeDtypeStruct((1, TOK, QCOLS), B...  72.4 us
    unnamed x2, local copies, waits for them, and re-layouts  3.93 us

profile of v2, /device:TPU:64, one launch (start us, length us, event | category | flops | bytes accessed | tf_op | source)
XLA Modules:
  0.0 82.2 jit_solution(6880569870715719952)
XLA Ops:
  0.7 0.8 lt.39
  1.4 0.5 convert_reduce_fusion.1
  1.9 0.3 select_reduce_fusion.1
  2.2 1.1 %select_reduce_fusion = s32[16,32]{1,0:T(8,128)S(1)} fusion(s32[512]{0:T(512)S(1)} %fusion.7, s32[16,32]{1,0:T(8,128)S(1)} %multiply_add_fusion, s32[512]{0:T(512)} %param.30), kind=kLoop, calls=%fused_computation | loop fusion | flops 785920 | bytes 8192 | tf_op jit(solution)/shard_map/reduce_sum | solution.py:419
  3.4 0.5 convert_reduce_fusion
  3.9 0.6 pad_add_fusion.lists
  4.5 1.4 %fusion.vec = f32[74,128]{1,0:T(8,128)} fusion(bf16[128]{0:T(256)(128)(2,1)} %param.23, bf16[128]{0:T(256)(128)(2,1)} %param.22, bf16[1024]{0:T(1024)(128)(2,1)} %param.21, bf16[8192]{0:T(1024)(128)(2,1)} %param.17), kind=kLoop, calls=%fused_computation.6 | loop fusion | flops 85248 | bytes 56832 | tf_op jit(solution)/shard_map/convert_element_type | solution.py:428
  5.9 72.4 %layer.1 = (bf16[1,512,1024]{2,1,0:T(8,128)(2,1)}, bf16[32,1,2,16,128]{4,3,2,1,0:T(8,128)(2,1)}) custom-call(s32[4]{0:T(128)} %ids.1, s32[1,3]{1,0:T(1,128)} %lengths.1, s32[2,16,32]{2,1,0:T(8,128)} %pad_add_fusion.lists, bf16[1,512,8192]{2,1,0:T(8,128)(2,1)} %tokens.1, f32[74,128]{1,0:T(8,128)} %fusion.vec, bf16[8192,1024]{1,0:T(8,128)(2,1)} %wq.1, ...), custom_call_target="tpu_custom_call" | custom-call | tf_op jit(solution)/shard_map/layer/pallas_call | solution.py:469
  78.3 2.3 %copy.20 = bf16[1,512,1024]{2,1,0:T(8,128)(2,1)} copy(bf16[1,512,1024]{2,1,0:T(8,128)(2,1)} %get-tuple-element.4) | data formatting | bytes 2097152
  80.5 1.7 %copy.21 = bf16[32,1,2,16,128]{4,3,2,1,0:T(8,128)(2,1)} copy(bf16[32,1,2,16,128]{4,3,2,1,0:T(8,128)(2,1)} %get-tuple-element.5) | data formatting | bytes 524288
  (4 shorter events, 0.0 us)

commit v3 on v2

--- a/solution.py
+++ b/solution.py
@@ -41,14 +41,14 @@
 
 
 def kernel(
-    ids, lengths, lists, tokens, vec, wq, wk, wv, down, upq, upk, upv, rope,
+    ids, lengths, tokens, gain, wq, wk, wv, bq, bk, bv, down, upq, upk, upv, table, rope,
     out, store,
-    x, wkv_b, wq_b, acc_kv, acc_q, sq, rsb, vecb, rope_b, cosb, sinb,
-    r1, r1u, st, stu, fac, upkv, zst, zr, zs, zf,
-    kvo, kvp, pst, prv, qx, kx, vx, top_b, sum_b,
-    tok_sem, wkv_sem, wq_sem, misc, own_u,
-    s1, s1u, s2, s2u, srs, sag, skv, spg,
-    v1, v1u, v2, v2u, vrs, vag, vkv, vpg,
+    x, wkv_b, wq_b, acc_kv, acc_q, sq, rsb, gain_b, bq_b, bk_b, bv_b, table_b, vecb, list_v, list_s, rope_b, cosb, sinb,
+    r1, r1u, st, stu, fac, upkv, zst, zr, zs, zf, zp,
+    kvo, kvb, kvp, pst, prv, qx, kx, vx, top_b, sum_b,
+    tok_sem, wkv_sem, wq_sem, misc,
+    s1, s1u, s2, s2u, srs, sag, skv, szp, spg,
+    v1, v1u, v2, v2u, vrs, vag, vkv, vzp, vpg,
 ):
     me_p = lax.axis_index("pool")
     me_g = lax.axis_index("group")
@@ -71,7 +71,10 @@
     def wq_copy(j):
         return pltpu.make_async_copy(wq.at[:, pl.ds(j * 256, 256)], wq_b.at[j], wq_sem.at[j])
 
-    vec_copy = pltpu.make_async_copy(vec, vecb, misc.at[0])
+    small = [
+        pltpu.make_async_copy(src, dst, misc.at[2 + n])
+        for n, (src, dst) in enumerate(((gain, gain_b), (bq, bq_b), (bk, bk_b), (bv, bv_b), (table, table_b)))
+    ]
     rope_copy = pltpu.make_async_copy(rope, rope_b, misc.at[1])
 
     upkv[...] = jnp.zeros_like(upkv)
@@ -94,7 +97,8 @@
     def _(i):
         pl.semaphore_signal(barrier, inc=1, device_id=(me_p, me_g, around(i)), device_id_type=MESH)
 
-    vec_copy.start()
+    for cp in small:
+        cp.start()
     for c in range(2):
         tok_copy(c).start()
         wkv_start(c)
@@ -115,6 +119,18 @@
             device_id=(dp, dg, dt), device_id_type=MESH,
         )
 
+    for n, src in enumerate((upk, upv)):
+        for dp in range(POOL):
+            dest = dp * GROUP + n
+
+            @pl.when(dest != owner)
+            def _():
+                remote(src.at[:, pl.ds(dp * 16, 16), :], r1u.at[mine2], s1u, v1u, dp, n, me_t).start()
+
+        @pl.when(me_g == n)
+        def _():
+            pltpu.make_async_copy(src.at[:, rows_of(me_p), :], r1u.at[mine2], v1u).start()
+
     @pl.loop(1, OWNERS)
     def _(i):
         dp, dg = plane(i)
@@ -124,18 +140,6 @@
 
     pltpu.make_async_copy(down.at[:, :, rows_of(me_p), cols_of(me_g)], r1.at[mine2, pl.ds(0, 3)], v1).start()
     pltpu.make_async_copy(upq.at[:, rows_of(me_p), cols_of(me_g)], r1.at[mine2, 3], v1).start()
-
-    for n, src in enumerate((upk, upv)):
-        for dp in range(POOL):
-            dest = dp * GROUP + n
-
-            @pl.when(dest != owner)
-            def _():
-                remote(src.at[:, pl.ds(dp * 16, 16), :], r1u.at[mine2], s1u, v1u, dp, n, me_t).start()
-
-        @pl.when(me_g == n)
-        def _():
-            pltpu.make_async_copy(src.at[:, rows_of(me_p), :], r1u.at[mine2], v1u).start()
 
     for c in range(2, 8):
         tok_copy(c).start()
@@ -146,7 +150,13 @@
 
     sq[...] = jnp.zeros_like(sq)
     acc_kv[...] = jnp.zeros_like(acc_kv)
-    vec_copy.wait()
+    for cp in small:
+        cp.wait()
+    for c in range(8):
+        vecb[pl.ds(c * 8, 8), :] = gain_b[pl.ds(c * CHUNK, CHUNK)].astype(F32).reshape(8, HEAD)
+    vecb[pl.ds(64, 8), :] = bq_b[...].astype(F32).reshape(8, HEAD)
+    vecb[pl.ds(72, 1), :] = bk_b[...].astype(F32).reshape(1, HEAD)
+    vecb[pl.ds(73, 1), :] = bv_b[...].astype(F32).reshape(1, HEAD)
 
     @pl.loop(0, 8)
     def _(c):
@@ -169,6 +179,9 @@
     mean = jnp.sum(sq[...], axis=1, keepdims=True) * (1.0 / WIDTH)
     rsb[...] = jnp.broadcast_to(lax.rsqrt(mean + EPS), (TOK, HEAD))
 
+    def bias(n):
+        return vecb[pl.ds(64 + n, 1), :]
+
     def q_tile(j):
         wq_copy(j).wait()
         cols = pl.ds(j * 256, 256)
@@ -178,13 +191,47 @@
         def _(c):
             acc_q[:, cols] += dot(x[c], wq_b[j, chunk(c), :])
 
+    kv_base = acc_kv[...] * jnp.concatenate([rsb[...], rsb[...]], axis=1)
+    kv_base = kv_base + jnp.concatenate([bias(8), bias(9)], axis=1)
+    acc_kv[...] = kv_base
+    kvb[...] = kv_base.astype(BF)
+
+    def make_lists():
+        shape = (32, HEAD)
+        list_v[...] = jnp.zeros_like(list_v)
+        sub = lax.broadcasted_iota(jnp.int32, shape, 0)
+        lan = lax.broadcasted_iota(jnp.int32, shape, 1)
+        slots = table_b[...].reshape(4, HEAD)
+        wide = [jnp.broadcast_to(slots[r : r + 1, :], shape) for r in range(4)]
+        mine = jnp.where(me_g < 2, jnp.where(me_g == 0, wide[0], wide[1]), jnp.where(me_g == 2, wide[2], wide[3]))
+        first = me_p * 32
+
+        def column(v, where):
+            return jnp.sum(jnp.where(where, v, 0), axis=1, keepdims=True)
+
+        def row(v, where):
+            return jnp.sum(jnp.where(where, v, 0), axis=0, keepdims=True)
+
+        own = column(mine, lan == sub + first)
+        inside = (lan >= first) & (lan < first + 32)
+        order = column(1, inside & (mine < own))
+        list_v[pl.ds(0, 1), :] = row(sub, order == lan)
+        source = jnp.zeros((32, 1), jnp.int32)
+        for r in range(4):
+            source = source + column(lan // 32 * GROUP + r, wide[r] == sub + owner * 32)
+        as_row = row(jnp.broadcast_to(source, shape), lan == sub)
+        item = source * 2 + column(1, (as_row == source) & (lan < sub))
+        list_v[pl.ds(1, 1), :] = row(jnp.broadcast_to(item, shape), lan == sub)
+        pltpu.make_async_copy(list_v, list_s, misc.at[0]).start()
+
     q_tile(0)
     q_tile(1)
-    q_tile(2)
 
     arrived(r1, v1)
     for g in range(GROUP):
-        st[g] = r1[ids[g]]
+        st[g, pl.ds(0, 2)] = r1[ids[g], pl.ds(1, 2)]
+        st[g, 2] = r1[ids[g], 0]
+        st[g, 3] = r1[ids[g], 3]
 
     @pl.loop(1, OWNERS)
     def _(i):
@@ -194,7 +241,7 @@
     pltpu.make_async_copy(st.at[me_g], fac.at[:, rows_of(me_p), cols_of(me_g)], v2).start()
 
     def up_place(n):
-        first = RANK * (n + 1) + me_p * 16
+        first = RANK * n + me_p * 16
         return upkv.at[pl.ds(pl.multiple_of(first, 16), 16), pl.ds(n * HEAD, HEAD)]
 
     for n in range(2):
@@ -212,12 +259,51 @@
 
             pltpu.make_async_copy(stu.at[me_g], up_place(n), v2u.at[n]).start()
 
+    q_tile(2)
+    make_lists()
+
+    arrived(fac, v2)
+
+    def ahead(step):
+        return remote(kvb, kvp.at[2 - step], skv.at[step - 1], vkv.at[step - 1], me_p + step, me_g, me_t)
+
+    def ahead_z(step):
+        return remote(
+            zf.at[:, :, pl.ds(0, HEAD)], zp.at[2 - step], szp.at[step - 1], vzp.at[step - 1], me_p + step, me_g, me_t
+        )
+
+    for step in (1, 2):
+
+        @pl.when(me_p < POOL - step)
+        def _():
+            ahead(step).start()
+
+    z = dot_t(x[me_t], fac[...].reshape(4 * RANK, CHUNK))
+    zst[...] = z.astype(BF).reshape(TENSOR, TOK // TENSOR, 4 * RANK)
+
+    @pl.loop(1, TENSOR)
+    def _(i):
+        dt = around(i)
+        remote(zst.at[dt], zr.at[i - 1], srs, vrs, me_p, me_g, dt).start()
+
+    q_tile(3)
+    arrived(zr, vrs)
+    total = zst[me_t].astype(F32)
+    for i in range(TENSOR - 1):
+        total = total + zr[i].astype(F32)
+    mine = rsb[pl.ds(pl.multiple_of(me_t * 64, 64), 64), :] * ADAPTER_SCALE
+    zs[...] = (total * jnp.concatenate([mine, mine], axis=1)).astype(BF)
+
+    @pl.loop(1, TENSOR)
+    def _(i):
+        remote(zs, zf.at[me_t], sag, vag, me_p, me_g, around(i)).start()
+
+    pltpu.make_async_copy(zs, zf.at[me_t], vag).start()
     rope_copy.wait()
     start1 = lengths[0, 0]
     start2 = lengths[0, 0] + lengths[0, 1]
     lane = lax.broadcasted_iota(jnp.int32, (TOK, HEAD), 1)
     low = lane < HEAD // 2
-    token = me_p * TOK + lax.broadcasted_iota(jnp.int32, (TOK, HEAD), 0)
 
     def both(row, low_mask):
         turned = pltpu.roll(row, HEAD // 2, 1)
@@ -230,16 +316,21 @@
 
     c1, n1 = start_row(start1)
     c2, n2 = start_row(start2)
-    tc, tn = both(rope_b[pl.ds(pl.multiple_of(me_p * TOK, TOK), TOK), :], low)
-    in1 = token >= start1
-    in2 = token >= start2
-    sc = jnp.where(in2, c2[0:1, :], jnp.where(in1, c1[0:1, :], 1.0))
-    sn = jnp.where(in2, n2[0:1, :], jnp.where(in1, n1[0:1, :], 0.0))
-    cosb[...] = tc * sc + tn * sn
-    swung = tn * sc - tc * sn
-    sinb[...] = jnp.where(low, -swung, swung)
-
-    segment = in1.astype(jnp.int32) + in2.astype(jnp.int32)
+
+    def rotation(n):
+        first = (me_p + (n - 2)) * TOK
+        token = first + lax.broadcasted_iota(jnp.int32, (TOK, HEAD), 0)
+        tc, tn = both(rope_b[pl.ds(pl.multiple_of(first, TOK), TOK), :], low)
+        in1 = token >= start1
+        in2 = token >= start2
+        sc = jnp.where(in2, c2[0:1, :], jnp.where(in1, c1[0:1, :], 1.0))
+        sn = jnp.where(in2, n2[0:1, :], jnp.where(in1, n1[0:1, :], 0.0))
+        cosb[n] = tc * sc + tn * sn
+        swung = tn * sc - tc * sn
+        sinb[n] = jnp.where(low, -swung, swung)
+        return in1.astype(jnp.int32) + in2.astype(jnp.int32)
+
+    segment = rotation(2)
     marks = jnp.where((lane < 4) & (lane != segment), MASKED, 0.0).astype(BF)
     for h in range(HEADS):
         qx[h, :, pl.ds(HEAD, HEAD)] = marks
@@ -249,57 +340,41 @@
     kx[pl.ds(HEAD, HEAD), :] = (mark_row == kseg).astype(F32).astype(BF)
     for n in range(3):
         vx[n, :, pl.ds(HEAD, HEAD)] = jnp.ones((TOK, HEAD), BF)
-
-    arrived(fac, v2)
-    z = dot_t(x[me_t], fac[...].reshape(4 * RANK, CHUNK))
-    zst[...] = z.astype(BF).reshape(TENSOR, TOK // TENSOR, 4 * RANK)
-
-    @pl.loop(1, TENSOR)
-    def _(i):
-        dt = around(i)
-        remote(zst.at[dt], zr.at[i - 1], srs, vrs, me_p, me_g, dt).start()
-
-    q_tile(3)
-    arrived(zr, vrs)
-    total = zst[me_t].astype(F32)
-    for i in range(TENSOR - 1):
-        total = total + zr[i].astype(F32)
-    zs[...] = total.astype(BF)
-
-    @pl.loop(1, TENSOR)
-    def _(i):
-        remote(zs, zf.at[me_t], sag, vag, me_p, me_g, around(i)).start()
-
-    pltpu.make_async_copy(zs, zf.at[me_t], vag).start()
     for n in range(2):
-        arrived(upkv.at[pl.ds(RANK * (n + 1), RANK), pl.ds(n * HEAD, HEAD)], v2u.at[n])
+
+        @pl.when(me_p + n >= 2)
+        def _():
+            rotation(n)
+
+    for n in range(2):
+        arrived(upkv.at[pl.ds(RANK * n, RANK), pl.ds(n * HEAD, HEAD)], v2u.at[n])
     arrived(zf, vag)
-    low_rank = zf[...].reshape(TOK, 4 * RANK)
-
-    def rotated(v):
-        return v * cosb[...] + pltpu.roll(v, HEAD // 2, 1) * sinb[...]
-
-    def bias(n):
-        return vecb[pl.ds(64 + n, 1), :]
-
-    kv = acc_kv[...] + ADAPTER_SCALE * dot(low_rank, upkv[...])
-    key = rotated(kv[:, :HEAD] * rsb[...] + bias(8)).astype(BF)
-    value = (kv[:, HEAD:] * rsb[...] + bias(9)).astype(BF)
+    for step in (1, 2):
+
+        @pl.when(me_p < POOL - step)
+        def _():
+            ahead_z(step).start()
+
+    def rotated(v, n):
+        return v * cosb[n] + pltpu.roll(v, HEAD // 2, 1) * sinb[n]
+
+    def finish(n, base, z):
+        kv = base + dot(z, upkv[...])
+        key = rotated(kv[:, :HEAD], n).astype(BF)
+        value = kv[:, HEAD:].astype(BF)
+        kx[pl.ds(0, HEAD), pl.ds(n * TOK, TOK)] = key.T
+        vx[n, :, pl.ds(0, HEAD)] = value
+        return key, value
+
+    key, value = finish(2, acc_kv[...], zf[:, :, pl.ds(0, HEAD)].reshape(TOK, HEAD))
     kvo[0] = key.reshape(TOK // PAGE, PAGE, HEAD)
     kvo[1] = value.reshape(TOK // PAGE, PAGE, HEAD)
 
-    def ahead(step):
-        return remote(kvo, kvp.at[2 - step], skv.at[step - 1], vkv.at[step - 1], me_p + step, me_g, me_t)
-
-    for step in (1, 2):
-
-        @pl.when(me_p < POOL - step)
-        def _():
-            ahead(step).start()
+    pltpu.make_async_copy(list_v, list_s, misc.at[0]).wait()
 
     @pl.loop(0, 2 * OWNERS)
     def _(n):
-        page = lists[0, me_g * POOL + me_p, n]
+        page = jnp.clip(list_s[0, n], 0, 31)
         pst[n, 0] = kvo[0, page]
         pst[n, 1] = kvo[1, page]
 
@@ -312,14 +387,11 @@
     pltpu.make_async_copy(pst.at[mine2], prv.at[mine2], vpg).start()
 
     for j in range(4):
-        q = acc_q[:, pl.ds(j * 256, 256)] + ADAPTER_SCALE * dot(low_rank[:, :RANK], fac[3, :, pl.ds(j * 256, 256)])
+        low_rank = dot(zf[:, :, pl.ds(HEAD, HEAD)].reshape(TOK, HEAD)[:, :RANK], fac[3, :, pl.ds(j * 256, 256)])
         for h in range(2):
-            head = q[:, h * HEAD : (h + 1) * HEAD] * rsb[...] + bias(2 * j + h)
-            qx[2 * j + h, :, pl.ds(0, HEAD)] = (rotated(head) * (HEAD**-0.5 * math.log2(math.e))).astype(BF)
-
-    def place(n, ref):
-        kx[pl.ds(0, HEAD), pl.ds(n * TOK, TOK)] = ref[0].reshape(TOK, HEAD).T
-        vx[n, :, pl.ds(0, HEAD)] = ref[1].reshape(TOK, HEAD)
+            head = acc_q[:, pl.ds(j * 256 + h * HEAD, HEAD)] * rsb[...] + bias(2 * j + h)
+            head = head + low_rank[:, h * HEAD : (h + 1) * HEAD]
+            qx[2 * j + h, :, pl.ds(0, HEAD)] = (rotated(head, 2) * (HEAD**-0.5 * math.log2(math.e))).astype(BF)
 
     causal = lax.broadcasted_iota(jnp.int32, (QB, QB), 0) >= lax.broadcasted_iota(jnp.int32, (QB, QB), 1)
 
@@ -342,9 +414,7 @@
         top_b[h, rows, :] = wide
 
     upper, lower, every = pl.ds(0, QB), pl.ds(QB, QB), pl.ds(0, TOK)
-    place(2, kvo)
-
-    @pl.loop(0, HEADS)
+    @pl.loop(0, HEADS, unroll=2)
     def _(h):
         attend(h, upper, 2, 0, QB, True)
         attend(h, lower, 2, 0, TOK, True)
@@ -352,23 +422,25 @@
     @pl.when(me_p >= 1)
     def _():
         ahead(1).wait_recv()
-        place(1, kvp.at[1])
-
-        @pl.loop(0, HEADS)
+        ahead_z(1).wait_recv()
+        finish(1, kvp[1].astype(F32), zp[1].reshape(TOK, HEAD))
+
+        @pl.loop(0, HEADS, unroll=2)
         def _(h):
             attend(h, every, 1, 0, TOK, False)
 
     @pl.when(me_p >= 2)
     def _():
         ahead(2).wait_recv()
-        place(0, kvp.at[0])
-
-        @pl.loop(0, HEADS)
+        ahead_z(2).wait_recv()
+        finish(0, kvp[0].astype(F32), zp[0].reshape(TOK, HEAD))
+
+        @pl.loop(0, HEADS, unroll=2)
         def _(h):
             attend(h, upper, 0, 0, TOK, False)
             attend(h, lower, 0, QB, QB, False)
 
-    @pl.loop(0, HEADS)
+    @pl.loop(0, HEADS, unroll=2)
     def _(h):
         both_parts = sum_b[h]
         out[0, :, pl.ds(pl.multiple_of(h * HEAD, HEAD), HEAD)] = (both_parts[:, :HEAD] / both_parts[:, HEAD:]).astype(BF)
@@ -377,7 +449,7 @@
 
     @pl.loop(0, 2 * OWNERS)
     def _(n):
-        store[n, 0] = prv[lists[1, owner, n]]
+        store[n, 0] = prv[jnp.clip(list_s[1, n], 0, 31)]
 
     arrived(r1.at[pl.ds(0, 2 * (OWNERS - 1))], s1)
     arrived(r1.at[pl.ds(0, OWNERS - 1)], s2)
@@ -399,6 +471,7 @@
         @pl.when(me_p < POOL - step)
         def _():
             ahead(step).wait_send()
+            ahead_z(step).wait_send()
 
 
 def rope_table():
@@ -408,24 +481,9 @@
     return np.concatenate([np.cos(angle), np.sin(angle)], axis=1).astype(np.float32)
 
 
-def page_lists(table):
-    slots = table.reshape(16, 32)
-    number = jnp.arange(32, dtype=jnp.int32)
-    order = jnp.sum((slots[:, None, :] < slots[:, :, None]).astype(jnp.int32), axis=2)
-    send = jnp.sum(jnp.where(order[:, None, :] == number[None, :, None], number[None, None, :], 0), axis=2)
-    pages = jnp.arange(512, dtype=jnp.int32)
-    sources = (pages % 128) // 32 * GROUP + pages // 128
-    wanted = pages.reshape(16, 32)
-    source = jnp.sum(jnp.where(table[None, None, :] == wanted[:, :, None], sources[None, None, :], 0), axis=2)
-    earlier = (source[:, None, :] == source[:, :, None]) & (number[None, None, :] < number[None, :, None])
-    recv = source * 2 + jnp.sum(earlier.astype(jnp.int32), axis=2)
-    return jnp.stack([send, recv])
-
-
 def per_device(
     tokens, gain, wq, wk, wv, bq, bk, bv, down, upq, upk, upv, ids, lengths, table
 ):
-    vec = jnp.concatenate([gain, bq, bk, bv]).astype(F32).reshape(74, HEAD)
     smem = pl.BlockSpec(memory_space=pltpu.SMEM)
     vmem = pl.BlockSpec(memory_space=pltpu.VMEM)
     hbm = pl.BlockSpec(memory_space=pl.ANY)
@@ -439,22 +497,31 @@
         V((TOK, QCOLS), F32),
         V((TOK, HEAD), F32),
         V((TOK, HEAD), F32),
+        V((WIDTH,), BF),
+        V((QCOLS,), BF),
+        V((HEAD,), BF),
+        V((HEAD,), BF),
+        V((512,), jnp.int32),
         V((74, HEAD), F32),
+        V((8, HEAD), jnp.int32),
+        pltpu.SMEM((8, HEAD), jnp.int32),
         V((2048, HEAD), F32),
-        V((TOK, HEAD), F32),
-        V((TOK, HEAD), F32),
+        V((3, TOK, HEAD), F32),
+        V((3, TOK, HEAD), F32),
         V((32, 4, 16, 256), BF),
         V((32, 16, HEAD), BF),
         V((4, 4, 16, 256), BF),
         V((4, 16, HEAD), BF),
         V((4, RANK, CHUNK), BF),
-        V((4 * RANK, 256), BF),
+        V((2 * RANK, 256), BF),
         V((8, 64, 256), BF),
         V((7, 64, 256), BF),
         V((64, 256), BF),
         V((8, 64, 256), BF),
+        V((2, 8, 64, HEAD), BF),
         V((2, 32, PAGE, HEAD), BF),
-        V((2, 2, 32, PAGE, HEAD), BF),
+        V((TOK, 256), BF),
+        V((2, TOK, 256), BF),
         V((32, 2, PAGE, HEAD), BF),
         V((32, 2, PAGE, HEAD), BF),
         V((HEADS, TOK, 2 * HEAD), BF),
@@ -462,9 +529,9 @@
         V((3, TOK, 2 * HEAD), BF),
         V((HEADS, TOK, HEAD), F32),
         V((HEADS, TOK, 2 * HEAD), F32),
-        D((8,)), D((8,)), D((4,)), D((2,)), D,
-        D, D, D, D, D, D, D((2,)), D,
-        D, D, D, D((2,)), D, D, D((2,)), D,
+        D((8,)), D((8,)), D((4,)), D((7,)),
+        D, D, D, D, D, D, D((2,)), D((2,)), D,
+        D, D, D, D((2,)), D, D, D((2,)), D((2,)), D,
     ]
     return pl.pallas_call(
         kernel,
@@ -472,14 +539,14 @@
             jax.ShapeDtypeStruct((1, TOK, QCOLS), BF),
             jax.ShapeDtypeStruct((32, 1, 2, PAGE, HEAD), BF),
         ),
-        in_specs=[smem, smem, smem] + [hbm] * 10,
+        in_specs=[smem, smem] + [hbm] * 14,
         out_specs=(vmem, vmem),
         scratch_shapes=scratch,
         compiler_params=pltpu.CompilerParams(
             collective_id=0, has_side_effects=True, vmem_limit_bytes=60 * 1024 * 1024
         ),
         name="layer",
-    )(ids, lengths, page_lists(table), tokens, vec, wq, wk, wv, down, upq, upk, upv, jnp.asarray(rope_table()))
+    )(ids, lengths, tokens, gain, wq, wk, wv, bq, bk, bv, down, upq, upk, upv, table, jnp.asarray(rope_table()))
 
 
 def solution(mesh):

time: 82.6 us -> 68.9 us (0.83)
  Pallas kernels: 72.4 us -> 64.2 us
  other arithmetic: 4.44 us -> 0 us
    pallas_call x1, Pallas kernels: 72.4 us -> 64.2 us  [per_device(): pl.pallas_call(kernel, out_shape=(jax.ShapeDtypeStruct((1, TOK, QCOLS), B...]
    reduce_sum x4 -> x0, other arithmetic: 2.41 us -> none  [the longest x1 1.15 us: page_lists(): jnp.sum(jnp.where(table[None, None, :] == wanted[:, :, None], sources[Non...]
    convert_element_type x1 -> x0, other arithmetic: 1.39 us -> none  [per_device(): vec = jnp.concatenate([gain, bq, bk, bv]).astype(F32).reshape(74, HEAD)]
where the time goes in v3:
time: 68.9 us; the launch traced here: 68.7 us
  Pallas kernels  64.2 us (93%)
  local copies, waits for them, and re-layouts  3.93 us (6%)
    pallas_call x1, Pallas kernels, per_device(): pl.pallas_call(kernel, out_shape=(jax.ShapeDtypeStruct((1, TOK, QCOLS), B...  64.2 us
    unnamed x2, local copies, waits for them, and re-layouts  3.93 us

profile of v3, /device:TPU:64, one launch (start us, length us, event | category | flops | bytes accessed | tf_op | source)
XLA Modules:
  0.0 68.7 jit_solution(3421062684699199203)
XLA Ops:
  0.6 64.2 %layer.1 = (bf16[1,512,1024]{2,1,0:T(8,128)(2,1)}, bf16[32,1,2,16,128]{4,3,2,1,0:T(8,128)(2,1)}) custom-call(s32[4]{0:T(128)} %ids.1, s32[1,3]{1,0:T(1,128)} %lengths.1, bf16[1,512,8192]{2,1,0:T(8,128)(2,1)} %tokens.1, bf16[8192]{0:T(1024)(128)(2,1)} %gain.1, bf16[8192,1024]{1,0:T(8,128)(2,1)} %wq.1, bf16[8192,128]{1,0:T(8,128)(2,1)} %wk.1, ...), custom_call_target="tpu_custom_call" | custom-call | tf_op jit(solution)/shard_map/layer/pallas_call | solution.py:536
  64.8 2.3 %copy.20 = bf16[1,512,1024]{2,1,0:T(8,128)(2,1)} copy(bf16[1,512,1024]{2,1,0:T(8,128)(2,1)} %get-tuple-element.4) | data formatting | bytes 2097152
  67.1 1.7 %copy.21 = bf16[32,1,2,16,128]{4,3,2,1,0:T(8,128)(2,1)} copy(bf16[32,1,2,16,128]{4,3,2,1,0:T(8,128)(2,1)} %get-tuple-element.5) | data formatting | bytes 524288

commit v4 on v3

--- a/solution.py
+++ b/solution.py
@@ -338,8 +338,7 @@
     ktok = (me_p - 2) * TOK + lax.broadcasted_iota(jnp.int32, (HEAD, 3 * TOK), 1)
     kseg = (ktok >= start1).astype(jnp.int32) + (ktok >= start2).astype(jnp.int32)
     kx[pl.ds(HEAD, HEAD), :] = (mark_row == kseg).astype(F32).astype(BF)
-    for n in range(3):
-        vx[n, :, pl.ds(HEAD, HEAD)] = jnp.ones((TOK, HEAD), BF)
+    vx[:, pl.ds(HEAD, HEAD)] = jnp.ones((3 * TOK, HEAD), BF)
     for n in range(2):
 
         @pl.when(me_p + n >= 2)
@@ -363,7 +362,7 @@
         key = rotated(kv[:, :HEAD], n).astype(BF)
         value = kv[:, HEAD:].astype(BF)
         kx[pl.ds(0, HEAD), pl.ds(n * TOK, TOK)] = key.T
-        vx[n, :, pl.ds(0, HEAD)] = value
+        vx[pl.ds(n * TOK, TOK), pl.ds(0, HEAD)] = value
         return key, value
 
     key, value = finish(2, acc_kv[...], zf[:, :, pl.ds(0, HEAD)].reshape(TOK, HEAD))
@@ -393,57 +392,76 @@
             head = head + low_rank[:, h * HEAD : (h + 1) * HEAD]
             qx[2 * j + h, :, pl.ds(0, HEAD)] = (rotated(head, 2) * (HEAD**-0.5 * math.log2(math.e))).astype(BF)
 
-    causal = lax.broadcasted_iota(jnp.int32, (QB, QB), 0) >= lax.broadcasted_iota(jnp.int32, (QB, QB), 1)
-
-    def attend(h, rows, n, first, count, diagonal):
-        score = dot(qx[h, rows, :], kx[:, pl.ds(n * TOK + first, count)])
-        if diagonal:
-            last = jnp.where(causal, score[:, count - QB :], MASKED)
-            score = last if count == QB else jnp.concatenate([score[:, : count - QB], last], axis=1)
+    pair_rows = lax.rem(lax.broadcasted_iota(jnp.int32, (2 * QB, QB), 0), QB)
+    causal = pair_rows >= lax.broadcasted_iota(jnp.int32, (2 * QB, QB), 1)
+
+    def heads_of(step):
+        return pl.ds(2 * step[0], 2), pl.ds(step[1] * QB, QB)
+
+    def scores(step):
+        heads, rows = heads_of(step)
+        return dot(qx[heads, rows, :].reshape(2 * QB, 2 * HEAD), kx[:, pl.ds(step[2], step[3])])
+
+    def put(step, ratio):
+        heads, rows = heads_of(step)
+        for n in range(2):
+            out[0, rows, pl.ds((2 * step[0] + n) * HEAD, HEAD)] = ratio[n * QB : (n + 1) * QB].astype(BF)
+
+    def own_step(step, score):
+        heads, rows = heads_of(step)
+        count = step[3]
+        last = jnp.where(causal, score[:, count - QB :], MASKED)
+        score = last if count == QB else jnp.concatenate([score[:, : count - QB], last], axis=1)
         top = jnp.max(score, axis=1, keepdims=True)
-        if not diagonal:
-            before = top_b[h, rows, :]
-            top = jnp.maximum(before[:, :1], top)
         weight = jnp.exp2(score - top).astype(BF)
-        part = dot(weight, vx[n, pl.ds(first, count), :])
-        wide = jnp.broadcast_to(top, (top.shape[0], HEAD))
-        if not diagonal:
-            fade = jnp.exp2(before - wide)
-            part = part + sum_b[h, rows, :] * jnp.concatenate([fade, fade], axis=1)
-        sum_b[h, rows, :] = part
-        top_b[h, rows, :] = wide
-
-    upper, lower, every = pl.ds(0, QB), pl.ds(QB, QB), pl.ds(0, TOK)
-    @pl.loop(0, HEADS, unroll=2)
-    def _(h):
-        attend(h, upper, 2, 0, QB, True)
-        attend(h, lower, 2, 0, TOK, True)
-
-    @pl.when(me_p >= 1)
+        part = dot(weight, vx[pl.ds(step[2], count), :])
+        sum_b[heads, rows, :] = part.reshape(2, QB, 2 * HEAD)
+        top_b[heads, rows, :] = jnp.broadcast_to(top, (2 * QB, HEAD)).reshape(2, QB, HEAD)
+
+    def earlier_step(step, score):
+        heads, rows = heads_of(step)
+        before = top_b[heads, rows, :].reshape(2 * QB, HEAD)
+        top = jnp.maximum(before[:, :1], jnp.max(score, axis=1, keepdims=True))
+        weight = jnp.exp2(score - top).astype(BF)
+        part = dot(weight, vx[pl.ds(step[2], step[3]), :])
+        fade = jnp.exp2(before - top)
+        old = sum_b[heads, rows, :].reshape(2 * QB, 2 * HEAD)
+        put(step, (part[:, :HEAD] + old[:, :HEAD] * fade) / (part[:, HEAD:] + old[:, HEAD:] * fade))
+
+    def run(steps, act):
+        score = scores(steps[0])
+        for n, step in enumerate(steps):
+            following = scores(steps[n + 1]) if n + 1 < len(steps) else None
+            act(step, score)
+            score = following
+
+    pairs = range(HEADS // 2)
+    run([(h, b, 2 * TOK, (b + 1) * QB) for h in pairs for b in range(2)], own_step)
+
+    @pl.when(me_p == 0)
     def _():
-        ahead(1).wait_recv()
-        ahead_z(1).wait_recv()
-        finish(1, kvp[1].astype(F32), zp[1].reshape(TOK, HEAD))
-
-        @pl.loop(0, HEADS, unroll=2)
-        def _(h):
-            attend(h, every, 1, 0, TOK, False)
+        for h in pairs:
+            for b in range(2):
+                heads, rows = heads_of((h, b))
+                old = sum_b[heads, rows, :].reshape(2 * QB, 2 * HEAD)
+                put((h, b), old[:, :HEAD] / old[:, HEAD:])
+
+    def take(step):
+        ahead(step).wait_recv()
+        ahead_z(step).wait_recv()
+        n = 2 - step
+        finish(n, kvp[n].astype(F32), zp[n].reshape(TOK, HEAD))
+
+    @pl.when(me_p == 1)
+    def _():
+        take(1)
+        run([(h, b, TOK, TOK) for h in pairs for b in range(2)], earlier_step)
 
     @pl.when(me_p >= 2)
     def _():
-        ahead(2).wait_recv()
-        ahead_z(2).wait_recv()
-        finish(0, kvp[0].astype(F32), zp[0].reshape(TOK, HEAD))
-
-        @pl.loop(0, HEADS, unroll=2)
-        def _(h):
-            attend(h, upper, 0, 0, TOK, False)
-            attend(h, lower, 0, QB, QB, False)
-
-    @pl.loop(0, HEADS, unroll=2)
-    def _(h):
-        both_parts = sum_b[h]
-        out[0, :, pl.ds(pl.multiple_of(h * HEAD, HEAD), HEAD)] = (both_parts[:, :HEAD] / both_parts[:, HEAD:]).astype(BF)
+        take(1)
+        take(2)
+        run([(h, b, b * QB, 2 * TOK - b * QB) for h in pairs for b in range(2)], earlier_step)
 
     arrived(prv, vpg)
 
@@ -472,6 +490,18 @@
         def _():
             ahead(step).wait_send()
             ahead_z(step).wait_send()
+
+
+def hand_over(out, store, out_to, store_to, out_b, store_b, come, go):
+    parts = [(out.at[0, pl.ds(n * 128, 128)], out_b.at[pl.ds(n * 128, 128)], out_to.at[0, pl.ds(n * 128, 128)]) for n in range(4)]
+    parts.append((store, store_b, store_to))
+    for n, (src, held, _) in enumerate(parts):
+        pltpu.make_async_copy(src, held, come.at[n]).start()
+    for n, (src, held, dst) in enumerate(parts):
+        pltpu.make_async_copy(src, held, come.at[n]).wait()
+        pltpu.make_async_copy(held, dst, go.at[n]).start()
+    for n, (_, held, dst) in enumerate(parts):
+        pltpu.make_async_copy(held, dst, go.at[n]).wait()
 
 
 def rope_table():
@@ -526,14 +556,14 @@
         V((32, 2, PAGE, HEAD), BF),
         V((HEADS, TOK, 2 * HEAD), BF),
         V((2 * HEAD, 3 * TOK), BF),
-        V((3, TOK, 2 * HEAD), BF),
+        V((3 * TOK, 2 * HEAD), BF),
         V((HEADS, TOK, HEAD), F32),
         V((HEADS, TOK, 2 * HEAD), F32),
         D((8,)), D((8,)), D((4,)), D((7,)),
         D, D, D, D, D, D, D((2,)), D((2,)), D,
         D, D, D, D((2,)), D, D, D((2,)), D((2,)), D,
     ]
-    return pl.pallas_call(
+    made = pl.pallas_call(
         kernel,
         out_shape=(
             jax.ShapeDtypeStruct((1, TOK, QCOLS), BF),
@@ -547,6 +577,14 @@
         ),
         name="layer",
     )(ids, lengths, tokens, gain, wq, wk, wv, bq, bk, bv, down, upq, upk, upv, table, jnp.asarray(rope_table()))
+    return pl.pallas_call(
+        hand_over,
+        out_shape=tuple(jax.ShapeDtypeStruct(m.shape, m.dtype) for m in made),
+        in_specs=[hbm, hbm],
+        out_specs=(hbm, hbm),
+        scratch_shapes=[V((TOK, QCOLS), BF), V((32, 1, 2, PAGE, HEAD), BF), D((5,)), D((5,))],
+        name="hand_over",
+    )(*made)
 
 
 def solution(mesh):

time: 68.9 us -> 62.7 us (0.910)
  local copies, waits for them, and re-layouts: 3.93 us -> 0 us
  Pallas kernels: 64.2 us -> 61.7 us
    pallas_call x1, Pallas kernels: 64.2 us -> 59.7 us  [per_device(): pl.pallas_call(kernel, out_shape=(jax.ShapeDtypeStruct((1, TOK, QCOLS), B...]
    unnamed x2 -> x0, local copies, waits for them, and re-layouts: 3.93 us -> none
    pallas_call x0 -> x1, Pallas kernels: none -> 2.08 us  [per_device(): pl.pallas_call(hand_over, out_shape=tuple((jax.ShapeDtypeStruct(m.shape,...]
where the time goes in v4:
time: 62.7 us; the launch traced here: 62.5 us
  Pallas kernels  61.7 us (98%)
  between operations  0.81 us (1%)
    pallas_call x1, Pallas kernels, per_device(): pl.pallas_call(kernel, out_shape=(jax.ShapeDtypeStruct((1, TOK, QCOLS), B...  59.7 us
    pallas_call x1, Pallas kernels, per_device(): pl.pallas_call(hand_over, out_shape=tuple((jax.ShapeDtypeStruct(m.shape,...  2.08 us

profile of v4, /device:TPU:64, one launch (start us, length us, event | category | flops | bytes accessed | tf_op | source)
XLA Modules:
  0.0 62.5 jit_solution(17561615704418523776)
XLA Ops:
  0.6 59.7 %layer.1 = (bf16[1,512,1024]{2,1,0:T(8,128)(2,1)}, bf16[32,1,2,16,128]{4,3,2,1,0:T(8,128)(2,1)}) custom-call(s32[4]{0:T(128)} %ids.1, s32[1,3]{1,0:T(1,128)} %lengths.1, bf16[1,512,8192]{2,1,0:T(8,128)(2,1)} %tokens.1, bf16[8192]{0:T(1024)(128)(2,1)} %gain.1, bf16[8192,1024]{1,0:T(8,128)(2,1)} %wq.1, bf16[8192,128]{1,0:T(8,128)(2,1)} %wk.1, ...), custom_call_target="tpu_custom_call" | custom-call | tf_op jit(solution)/shard_map/layer/pallas_call | solution.py:566
  60.3 2.1 %hand_over.1 = (bf16[1,512,1024]{2,1,0:T(8,128)(2,1)}, bf16[32,1,2,16,128]{4,3,2,1,0:T(8,128)(2,1)}) custom-call(bf16[1,512,1024]{2,1,0:T(8,128)(2,1)} %get-tuple-element.4.out, bf16[32,1,2,16,128]{4,3,2,1,0:T(8,128)(2,1)} %get-tuple-element.5.store), custom_call_target="tpu_custom_call" | custom-call | tf_op jit(solution)/shard_map/hand_over/pallas_call | solution.py:580

commit v5 on v4

--- a/solution.py
+++ b/solution.py
@@ -41,12 +41,13 @@
 
 
 def kernel(
+    single,
     ids, lengths, tokens, gain, wq, wk, wv, bq, bk, bv, down, upq, upk, upv, table, rope,
     out, store,
     x, wkv_b, wq_b, acc_kv, acc_q, sq, rsb, gain_b, bq_b, bk_b, bv_b, table_b, vecb, list_v, list_s, rope_b, cosb, sinb,
-    r1, r1u, st, stu, fac, upkv, zst, zr, zs, zf, zp,
+    bank_b, bank_u, pick_b, pick_u, r1, r1u, st, stu, fac, upkv, zst, zr, zs, zf, zp,
     kvo, kvb, kvp, pst, prv, qx, kx, vx, top_b, sum_b,
-    tok_sem, wkv_sem, wq_sem, misc,
+    tok_sem, wkv_sem, wq_sem, misc, bank_sem,
     s1, s1u, s2, s2u, srs, sag, skv, szp, spg,
     v1, v1u, v2, v2u, vrs, vag, vkv, vzp, vpg,
 ):
@@ -97,12 +98,32 @@
     def _(i):
         pl.semaphore_signal(barrier, inc=1, device_id=(me_p, me_g, around(i)), device_id_type=MESH)
 
+    if single:
+        pltpu.make_async_copy(down, bank_b.at[:, pl.ds(0, 3)], bank_sem.at[0]).start()
+        pltpu.make_async_copy(upq, bank_b.at[:, 3], bank_sem.at[0]).start()
+        for n, src in enumerate((upk, upv)):
+            pltpu.make_async_copy(src, bank_u.at[n], bank_sem.at[1]).start()
     for cp in small:
         cp.start()
     for c in range(2):
         tok_copy(c).start()
         wkv_start(c)
 
+    per_owner = 1 if single else 2
+
+    def entry(g):
+        return lax.div(ids[g], 2) if single else ids[g]
+
+    if single:
+        slot = jnp.int32(0)
+        for g in range(GROUP):
+            slot = jnp.where(lax.div(ids[g], 2) == owner, lax.rem(ids[g], 2), slot)
+        arrived(bank_b, bank_sem.at[0])
+        arrived(bank_u, bank_sem.at[1])
+        pick_b[...] = bank_b[slot]
+        for n in range(2):
+            pick_u[n] = bank_u[n, slot]
+
     pl.semaphore_wait(barrier, OWNERS - 1 + TENSOR - 1)
 
     mine2 = pl.ds(owner * 2, 2)
@@ -119,27 +140,41 @@
             device_id=(dp, dg, dt), device_id_type=MESH,
         )
 
-    for n, src in enumerate((upk, upv)):
+    def main_parts(rows, cols):
+        if single:
+            return ((pick_b.at[:, rows, cols], r1.at[owner]),)
+        return (
+            (down.at[:, :, rows, cols], r1.at[mine2, pl.ds(0, 3)]),
+            (upq.at[:, rows, cols], r1.at[mine2, 3]),
+        )
+
+    def up_part(n, rows):
+        if single:
+            return pick_u.at[n, rows], r1u.at[owner]
+        return (upk, upv)[n].at[:, rows, :], r1u.at[mine2]
+
+    for n in range(2):
         for dp in range(POOL):
             dest = dp * GROUP + n
 
             @pl.when(dest != owner)
             def _():
-                remote(src.at[:, pl.ds(dp * 16, 16), :], r1u.at[mine2], s1u, v1u, dp, n, me_t).start()
+                src, dst = up_part(n, pl.ds(dp * 16, 16))
+                remote(src, dst, s1u, v1u, dp, n, me_t).start()
 
         @pl.when(me_g == n)
         def _():
-            pltpu.make_async_copy(src.at[:, rows_of(me_p), :], r1u.at[mine2], v1u).start()
+            src, dst = up_part(n, rows_of(me_p))
+            pltpu.make_async_copy(src, dst, v1u).start()
 
     @pl.loop(1, OWNERS)
     def _(i):
         dp, dg = plane(i)
-        rows, cols = rows_of(dp), cols_of(dg)
-        remote(down.at[:, :, rows, cols], r1.at[mine2, pl.ds(0, 3)], s1, v1, dp, dg, me_t).start()
-        remote(upq.at[:, rows, cols], r1.at[mine2, 3], s1, v1, dp, dg, me_t).start()
-
-    pltpu.make_async_copy(down.at[:, :, rows_of(me_p), cols_of(me_g)], r1.at[mine2, pl.ds(0, 3)], v1).start()
-    pltpu.make_async_copy(upq.at[:, rows_of(me_p), cols_of(me_g)], r1.at[mine2, 3], v1).start()
+        for src, dst in main_parts(rows_of(dp), cols_of(dg)):
+            remote(src, dst, s1, v1, dp, dg, me_t).start()
+
+    for src, dst in main_parts(rows_of(me_p), cols_of(me_g)):
+        pltpu.make_async_copy(src, dst, v1).start()
 
     for c in range(2, 8):
         tok_copy(c).start()
@@ -224,14 +259,15 @@
         list_v[pl.ds(1, 1), :] = row(jnp.broadcast_to(item, shape), lan == sub)
         pltpu.make_async_copy(list_v, list_s, misc.at[0]).start()
 
-    q_tile(0)
-    q_tile(1)
-
-    arrived(r1, v1)
+    if not single:
+        q_tile(0)
+        q_tile(1)
+
+    arrived(r1.at[pl.ds(0, per_owner * OWNERS)], v1)
     for g in range(GROUP):
-        st[g, pl.ds(0, 2)] = r1[ids[g], pl.ds(1, 2)]
-        st[g, 2] = r1[ids[g], 0]
-        st[g, 3] = r1[ids[g], 3]
+        st[g, pl.ds(0, 2)] = r1[entry(g), pl.ds(1, 2)]
+        st[g, 2] = r1[entry(g), 0]
+        st[g, 3] = r1[entry(g), 3]
 
     @pl.loop(1, OWNERS)
     def _(i):
@@ -248,9 +284,9 @@
 
         @pl.when(me_g == n)
         def _():
-            arrived(r1u, v1u)
+            arrived(r1u.at[pl.ds(0, per_owner * OWNERS)], v1u)
             for g in range(GROUP):
-                stu[g] = r1u[ids[g]]
+                stu[g] = r1u[entry(g)]
 
             @pl.loop(1, OWNERS)
             def _(i):
@@ -259,6 +295,9 @@
 
             pltpu.make_async_copy(stu.at[me_g], up_place(n), v2u.at[n]).start()
 
+    if single:
+        q_tile(0)
+        q_tile(1)
     q_tile(2)
     make_lists()
 
@@ -469,7 +508,7 @@
     def _(n):
         store[n, 0] = prv[jnp.clip(list_s[1, n], 0, 31)]
 
-    arrived(r1.at[pl.ds(0, 2 * (OWNERS - 1))], s1)
+    arrived(r1.at[pl.ds(0, per_owner * (OWNERS - 1))], s1)
     arrived(r1.at[pl.ds(0, OWNERS - 1)], s2)
     arrived(zr, srs)
     arrived(zr, sag)
@@ -477,12 +516,12 @@
 
     @pl.when(me_g < 2)
     def _():
-        arrived(r1u.at[pl.ds(0, 2 * 7)], s1u)
+        arrived(r1u.at[pl.ds(0, per_owner * 7)], s1u)
         arrived(r1u.at[pl.ds(0, OWNERS - 1)], s2u)
 
     @pl.when(me_g >= 2)
     def _():
-        arrived(r1u.at[pl.ds(0, 2 * 8)], s1u)
+        arrived(r1u.at[pl.ds(0, per_owner * 8)], s1u)
 
     for step in (1, 2):
 
@@ -538,6 +577,10 @@
         V((2048, HEAD), F32),
         V((3, TOK, HEAD), F32),
         V((3, TOK, HEAD), F32),
+        V((2, 4, RANK, CHUNK), BF),
+        V((2, 2, RANK, HEAD), BF),
+        V((4, RANK, CHUNK), BF),
+        V((2, RANK, HEAD), BF),
         V((32, 4, 16, 256), BF),
         V((32, 16, HEAD), BF),
         V((4, 4, 16, 256), BF),
@@ -559,24 +602,29 @@
         V((3 * TOK, 2 * HEAD), BF),
         V((HEADS, TOK, HEAD), F32),
         V((HEADS, TOK, 2 * HEAD), F32),
-        D((8,)), D((8,)), D((4,)), D((7,)),
+        D((8,)), D((8,)), D((4,)), D((7,)), D((2,)),
         D, D, D, D, D, D, D((2,)), D((2,)), D,
         D, D, D, D((2,)), D, D, D((2,)), D((2,)), D,
     ]
-    made = pl.pallas_call(
-        kernel,
-        out_shape=(
-            jax.ShapeDtypeStruct((1, TOK, QCOLS), BF),
-            jax.ShapeDtypeStruct((32, 1, 2, PAGE, HEAD), BF),
-        ),
-        in_specs=[smem, smem] + [hbm] * 14,
-        out_specs=(vmem, vmem),
-        scratch_shapes=scratch,
-        compiler_params=pltpu.CompilerParams(
-            collective_id=0, has_side_effects=True, vmem_limit_bytes=60 * 1024 * 1024
-        ),
-        name="layer",
-    )(ids, lengths, tokens, gain, wq, wk, wv, bq, bk, bv, down, upq, upk, upv, table, jnp.asarray(rope_table()))
+    def layer(single):
+        return pl.pallas_call(
+            functools.partial(kernel, single),
+            out_shape=(
+                jax.ShapeDtypeStruct((1, TOK, QCOLS), BF),
+                jax.ShapeDtypeStruct((32, 1, 2, PAGE, HEAD), BF),
+            ),
+            in_specs=[smem, smem] + [hbm] * 14,
+            out_specs=(vmem, vmem),
+            scratch_shapes=scratch,
+            compiler_params=pltpu.CompilerParams(
+                collective_id=1 if single else 0, has_side_effects=True, vmem_limit_bytes=60 * 1024 * 1024
+            ),
+            name="layer_single" if single else "layer",
+        )
+
+    both = jnp.any((ids[:, None] ^ ids[None, :]) == 1)
+    operands = (ids, lengths, tokens, gain, wq, wk, wv, bq, bk, bv, down, upq, upk, upv, table, jnp.asarray(rope_table()))
+    made = lax.cond(both, layer(False), layer(True), *operands)
     return pl.pallas_call(
         hand_over,
         out_shape=tuple(jax.ShapeDtypeStruct(m.shape, m.dtype) for m in made),

time: 62.7 us -> 58.4 us (0.931)
  Pallas kernels: 61.7 us -> 54.8 us
  other arithmetic: 0 us -> 1.44 us
  between operations: 0.81 us -> 1.51 us
    pallas_call x1, Pallas kernels: 59.7 us -> 53.6 us  [per_device(): made = lax.cond(both, layer(False), layer(True), *operands)]
    reduce_or x0 -> x1, other arithmetic: none -> 1.44 us  [per_device(): both = jnp.any(ids[:, None] ^ ids[None, :] == 1)]
    pallas_call x1, Pallas kernels: 2.08 us -> 1.23 us  [per_device(): pl.pallas_call(hand_over, out_shape=tuple((jax.ShapeDtypeStruct(m.shape,...]
where the time goes in v5:
time: 58.4 us; the launch traced here: 58.3 us
  Pallas kernels  54.8 us (94%)
  between operations  1.51 us (3%)
  other arithmetic  1.44 us (2%)
    pallas_call x1, Pallas kernels, per_device(): made = lax.cond(both, layer(False), layer(True), *operands)  53.6 us
    reduce_or x1, other arithmetic, per_device(): both = jnp.any(ids[:, None] ^ ids[None, :] == 1)  1.44 us
    pallas_call x1, Pallas kernels, per_device(): pl.pallas_call(hand_over, out_shape=tuple((jax.ShapeDtypeStruct(m.shape,...  1.23 us

profile of v5, /device:TPU:64, one launch (start us, length us, event | category | flops | bytes accessed | tf_op | source)
XLA Modules:
  0.0 58.3 jit_solution(13581658330076139863)
XLA Ops:
  0.6 1.4 %fusion = pred[]{:T(512)} fusion(s32[4]{0:T(128)} %param.30), kind=kLoop, calls=%fused_computation.1 | loop fusion | flops 47 | bytes 17 | tf_op jit(solution)/shard_map/reduce_or | solution.py:625
  2.7 54.1 %conditional.1 = ((bf16[1,512,1024]{2,1,0:T(8,128)(2,1)S(1)}, bf16[32,1,2,16,128]{4,3,2,1,0:T(8,128)(2,1)S(1)})) conditional(s32[]{:T(128)} %convert_element_type.3, (s32[4]{0:T(128)}, s32[1,3]{1,0:T(1,128)}, bf16[1,512,8192]{2,1,0:T(8,128)(2,1)}, bf16[8192]{0:T(1024)(128)(2,1)}, bf16[8192,1024]{1,0:T(8,128)(2,1)}, ...), branch_computations={%region_1.0_spmd, %region_2.0_spmd} | conditional | bytes 8 | solution.py:627
  2.7 53.6 %layer_single.1 = (bf16[1,512,1024]{2,1,0:T(8,128)(2,1)S(1)}, bf16[32,1,2,16,128]{4,3,2,1,0:T(8,128)(2,1)S(1)}) custom-call(s32[4]{0:T(128)} %get-tuple-element.64.ids, s32[1,3]{1,0:T(1,128)} %get-tuple-element.65.lengths, bf16[1,512,8192]{2,1,0:T(8,128)(2,1)} %get-tuple-element.66.tokens, bf16[8192]{0:T(1024)(128)(2,1)} %get-tuple-element.67.gain, ...), custom_call_target="tpu_custom_call" | custom-call | tf_op jit(solution)/shard_map/cond/branch_0_fun/layer_single/pallas_call | solution.py:627
  56.8 1.2 %hand_over.1 = (bf16[1,512,1024]{2,1,0:T(8,128)(2,1)}, bf16[32,1,2,16,128]{4,3,2,1,0:T(8,128)(2,1)}) custom-call(bf16[1,512,1024]{2,1,0:T(8,128)(2,1)S(1)} %get-tuple-element.100.out, bf16[32,1,2,16,128]{4,3,2,1,0:T(8,128)(2,1)S(1)} %get-tuple-element.101.store), custom_call_target="tpu_custom_call" | custom-call | tf_op jit(solution)/shard_map/hand_over/pallas_call | solution.py:628

commit v6 on v5

--- a/solution.py
+++ b/solution.py
@@ -78,31 +78,32 @@
     ]
     rope_copy = pltpu.make_async_copy(rope, rope_b, misc.at[1])
 
-    upkv[...] = jnp.zeros_like(upkv)
-
-    barrier = pltpu.get_barrier_semaphore()
-
-    def plane(i):
-        dest = lax.rem(owner + i, OWNERS)
-        return dest // GROUP, lax.rem(dest, GROUP)
-
-    def around(i):
-        return lax.rem(me_t + i, TENSOR)
-
-    @pl.loop(1, OWNERS)
-    def _(i):
-        dp, dg = plane(i)
-        pl.semaphore_signal(barrier, inc=1, device_id=(dp, dg, me_t), device_id_type=MESH)
-
-    @pl.loop(1, TENSOR)
-    def _(i):
-        pl.semaphore_signal(barrier, inc=1, device_id=(me_p, me_g, around(i)), device_id_type=MESH)
-
     if single:
         pltpu.make_async_copy(down, bank_b.at[:, pl.ds(0, 3)], bank_sem.at[0]).start()
         pltpu.make_async_copy(upq, bank_b.at[:, 3], bank_sem.at[0]).start()
         for n, src in enumerate((upk, upv)):
             pltpu.make_async_copy(src, bank_u.at[n], bank_sem.at[1]).start()
+
+    upkv[...] = jnp.zeros_like(upkv)
+
+    barrier = pltpu.get_barrier_semaphore()
+
+    def plane(i):
+        dest = lax.rem(owner + i, OWNERS)
+        return dest // GROUP, lax.rem(dest, GROUP)
+
+    def around(i):
+        return lax.rem(me_t + i, TENSOR)
+
+    @pl.loop(1, OWNERS)
+    def _(i):
+        dp, dg = plane(i)
+        pl.semaphore_signal(barrier, inc=1, device_id=(dp, dg, me_t), device_id_type=MESH)
+
+    @pl.loop(1, TENSOR)
+    def _(i):
+        pl.semaphore_signal(barrier, inc=1, device_id=(me_p, me_g, around(i)), device_id_type=MESH)
+
     for cp in small:
         cp.start()
     for c in range(2):
@@ -124,6 +125,13 @@
         for n in range(2):
             pick_u[n] = bank_u[n, slot]
 
+    for c in range(2, 8):
+        tok_copy(c).start()
+        wkv_start(c)
+    rope_copy.start()
+    for j in range(4):
+        wq_copy(j).start()
+
     pl.semaphore_wait(barrier, OWNERS - 1 + TENSOR - 1)
 
     mine2 = pl.ds(owner * 2, 2)
@@ -176,12 +184,6 @@
     for src, dst in main_parts(rows_of(me_p), cols_of(me_g)):
         pltpu.make_async_copy(src, dst, v1).start()
 
-    for c in range(2, 8):
-        tok_copy(c).start()
-        wkv_start(c)
-    rope_copy.start()
-    for j in range(4):
-        wq_copy(j).start()
 
     sq[...] = jnp.zeros_like(sq)
     acc_kv[...] = jnp.zeros_like(acc_kv)
@@ -325,19 +327,6 @@
         dt = around(i)
         remote(zst.at[dt], zr.at[i - 1], srs, vrs, me_p, me_g, dt).start()
 
-    q_tile(3)
-    arrived(zr, vrs)
-    total = zst[me_t].astype(F32)
-    for i in range(TENSOR - 1):
-        total = total + zr[i].astype(F32)
-    mine = rsb[pl.ds(pl.multiple_of(me_t * 64, 64), 64), :] * ADAPTER_SCALE
-    zs[...] = (total * jnp.concatenate([mine, mine], axis=1)).astype(BF)
-
-    @pl.loop(1, TENSOR)
-    def _(i):
-        remote(zs, zf.at[me_t], sag, vag, me_p, me_g, around(i)).start()
-
-    pltpu.make_async_copy(zs, zf.at[me_t], vag).start()
     rope_copy.wait()
     start1 = lengths[0, 0]
     start2 = lengths[0, 0] + lengths[0, 1]
@@ -384,6 +373,19 @@
         def _():
             rotation(n)
 
+    arrived(zr, vrs)
+    total = zst[me_t].astype(F32)
+    for i in range(TENSOR - 1):
+        total = total + zr[i].astype(F32)
+    mine = rsb[pl.ds(pl.multiple_of(me_t * 64, 64), 64), :] * ADAPTER_SCALE
+    zs[...] = (total * jnp.concatenate([mine, mine], axis=1)).astype(BF)
+
+    @pl.loop(1, TENSOR)
+    def _(i):
+        remote(zs, zf.at[me_t], sag, vag, me_p, me_g, around(i)).start()
+
+    pltpu.make_async_copy(zs, zf.at[me_t], vag).start()
+    q_tile(3)
     for n in range(2):
         arrived(upkv.at[pl.ds(RANK * n, RANK), pl.ds(n * HEAD, HEAD)], v2u.at[n])
     arrived(zf, vag)

time: 58.4 us -> 58.1 us (level)
  no operation moved by 1% of the time
where the time goes in v6:
time: 58.1 us; the launch traced here: 57.9 us
  Pallas kernels  54.4 us (94%)
  between operations  1.51 us (3%)
  other arithmetic  1.44 us (2%)
    pallas_call x1, Pallas kernels, per_device(): made = lax.cond(both, layer(False), layer(True), *operands)  53.2 us
    reduce_or x1, other arithmetic, per_device(): both = jnp.any(ids[:, None] ^ ids[None, :] == 1)  1.44 us
    pallas_call x1, Pallas kernels, per_device(): pl.pallas_call(hand_over, out_shape=tuple((jax.ShapeDtypeStruct(m.shape,...  1.23 us

profile of v6, /device:TPU:64, one launch (start us, length us, event | category | flops | bytes accessed | tf_op | source)
XLA Modules:
  0.0 57.9 jit_solution(5724921466972436540)
XLA Ops:
  0.6 1.4 %fusion = pred[]{:T(512)} fusion(s32[4]{0:T(128)} %param.30), kind=kLoop, calls=%fused_computation.1 | loop fusion | flops 47 | bytes 17 | tf_op jit(solution)/shard_map/reduce_or | solution.py:627
  2.7 53.7 %conditional.1 = ((bf16[1,512,1024]{2,1,0:T(8,128)(2,1)S(1)}, bf16[32,1,2,16,128]{4,3,2,1,0:T(8,128)(2,1)S(1)})) conditional(s32[]{:T(128)} %convert_element_type.3, (s32[4]{0:T(128)}, s32[1,3]{1,0:T(1,128)}, bf16[1,512,8192]{2,1,0:T(8,128)(2,1)}, bf16[8192]{0:T(1024)(128)(2,1)}, bf16[8192,1024]{1,0:T(8,128)(2,1)}, ...), branch_computations={%region_1.0_spmd, %region_2.0_spmd} | conditional | bytes 8 | solution.py:629
  2.7 53.2 %layer_single.1 = (bf16[1,512,1024]{2,1,0:T(8,128)(2,1)S(1)}, bf16[32,1,2,16,128]{4,3,2,1,0:T(8,128)(2,1)S(1)}) custom-call(s32[4]{0:T(128)} %get-tuple-element.64.ids, s32[1,3]{1,0:T(1,128)} %get-tuple-element.65.lengths, bf16[1,512,8192]{2,1,0:T(8,128)(2,1)} %get-tuple-element.66.tokens, bf16[8192]{0:T(1024)(128)(2,1)} %get-tuple-element.67.gain, ...), custom_call_target="tpu_custom_call" | custom-call | tf_op jit(solution)/shard_map/cond/branch_0_fun/layer_single/pallas_call | solution.py:629
  56.5 1.2 %hand_over.1 = (bf16[1,512,1024]{2,1,0:T(8,128)(2,1)}, bf16[32,1,2,16,128]{4,3,2,1,0:T(8,128)(2,1)}) custom-call(bf16[1,512,1024]{2,1,0:T(8,128)(2,1)S(1)} %get-tuple-element.100.out, bf16[32,1,2,16,128]{4,3,2,1,0:T(8,128)(2,1)S(1)} %get-tuple-element.101.store), custom_call_target="tpu_custom_call" | custom-call | tf_op jit(solution)/shard_map/hand_over/pallas_call | solution.py:630
